TPU v7x, 512 devices: a whole 4x4x16 slice. The times are simulated.
512 devices in a mesh: ctx: 16 (over z_lo, core), exp: 32 (over z_hi, x, y).
Axes of the slice: x: 4, y: 4, z: 16 (z_hi: 2, z_lo: 8; z = z_hi * 8 + z_lo), core: 2. Of those that a mesh axis runs over, the one named last changes fastest.
Arguments:
- query: bfloat16 [32, 2048, 4096], P('exp', 'ctx'), may hold values from -41 to 41
- keyval: bfloat16 [32, 2, 2048, 256], P('exp', None, 'ctx'), may hold values from -4 to 4
- doc_ids: int32 [32, 2048], P('exp', 'ctx'), may hold values from 0 to 5, never falling along the last dimension, each value on 1 to 1024 neighbouring positions
- route_ids: int32 [32, 2048], P('exp', 'ctx'), may hold values from 0 to 63
- combine: float32 [32, 2048], P('exp', 'ctx'), may hold values from 0.5 to 2
- w_gate_up: bfloat16 [32, 2, 1536, 4096], P('exp', None, 'ctx'), may hold values from -0.09375 to 0.09375
- w_down: bfloat16 [32, 1536, 4096], P('exp', None, 'ctx'), may hold values from -0.15625 to 0.15625
Outputs:
- layer_out: bfloat16 [32, 2048, 4096], P('exp', 'ctx')
All inputs are finite; a program needn't handle non-finite values.
Results may differ from a plain program's by a relative error of at most 0.024.
Values may be sent and summed in bfloat16 or wider, within the bound.
A program may use at most 128 MiB of HBM per device.

v0:
```python
import jax
import jax.numpy as jnp
from jax import lax
from jax.sharding import PartitionSpec as P

HD = 128
CAP = 2


neg_large = -1e30
norm_eps = 1e-06


def shifted(value, axis, by):
    length = lax.axis_size(axis)
    return lax.ppermute(value, axis, [(i, (i + by) % length) for i in range(length)])


def shards(query, keyval, doc_ids, route_ids, combine, w_gate_up, w_down):
    tok_rows = query.shape[1]
    feature_width = query.shape[2]
    kv_heads = keyval.shape[3] // HD
    head_group = feature_width // HD // kv_heads
    ctx_count = lax.axis_size("ctx")
    q_heads = query[0].reshape(tok_rows, kv_heads, head_group, HD)
    q_doc = doc_ids[0]
    score_scale = HD ** (-0.5)

    def attend(loop_carry, kv_pair):
        kv_piece, doc_piece = kv_pair
        rows_here = kv_piece.shape[2]
        key_rows = kv_piece[0, 0].reshape(rows_here, kv_heads, HD)
        value_rows = kv_piece[0, 1].reshape(rows_here, kv_heads, HD)
        allowed = doc_piece[0, 0][None, :] == q_doc[:, None]
        running_max, running_sum, running_out = loop_carry
        scores = (
            jnp.einsum("qhgd,khd->hgqk", q_heads, key_rows, preferred_element_type=jnp.float32)
            * score_scale
        )
        masked = jnp.where(allowed, scores, neg_large)
        fresh_max = jnp.maximum(running_max, jnp.max(masked, axis=-1))
        prob_block = jnp.where(allowed, jnp.exp(masked - fresh_max[..., None]), 0.0)
        rescale = jnp.exp(running_max - fresh_max)
        running_sum = running_sum * rescale + jnp.sum(prob_block, axis=-1)
        block_out = jnp.einsum(
            "hgqk,khd->hgqd",
            prob_block.astype(jnp.bfloat16),
            value_rows,
            preferred_element_type=jnp.float32,
        )
        return (fresh_max, running_sum, running_out * rescale[..., None] + block_out)

    start_state = (
        jnp.full((kv_heads, head_group, tok_rows), neg_large, jnp.float32),
        jnp.zeros((kv_heads, head_group, tok_rows), jnp.float32),
        jnp.zeros((kv_heads, head_group, tok_rows, HD), jnp.float32),
    )
    doc_keys = doc_ids.reshape(1, 1, tok_rows)

    def cycle_step(step_index, loop_state):
        loop_carry, kv_now, doc_now = loop_state
        loop_carry = attend(loop_carry, (kv_now, doc_now))
        kv_next, doc_next = shifted((kv_now, doc_now), "ctx", 1)
        return (loop_carry, kv_next, doc_next)

    loop_carry, kv_last, doc_last = lax.fori_loop(
        0, ctx_count - 1, cycle_step, (start_state, keyval, doc_keys)
    )
    running_max, running_sum, running_out = attend(loop_carry, (kv_last, doc_last))
    head_major = (running_out / running_sum[..., None]).astype(jnp.bfloat16)
    attended = head_major.transpose(2, 0, 1, 3).reshape(tok_rows, feature_width)
    flat_attended = attended.astype(jnp.float32)
    normed = (
        flat_attended
        * lax.rsqrt(jnp.mean(flat_attended * flat_attended, axis=-1, keepdims=True) + norm_eps)
    ).astype(jnp.bfloat16)
    expert_count = lax.axis_size("exp")
    token_ids = route_ids[0]
    onehot = (token_ids[:, None] == lax.iota(jnp.int32, expert_count)[None, :]).astype(jnp.int32)
    earlier = jnp.sum((jnp.cumsum(onehot, axis=0) - onehot) * onehot, axis=1)
    kept = (token_ids < expert_count) & (earlier < CAP)
    slot = jnp.where(kept, token_ids * CAP + earlier, -1)
    chooser = (lax.iota(jnp.int32, expert_count * CAP)[:, None] == slot[None, :]).astype(
        jnp.bfloat16
    )
    outgoing = jnp.dot(chooser, normed, preferred_element_type=jnp.float32).astype(jnp.bfloat16)
    outgoing = outgoing.reshape(expert_count, CAP, feature_width)
    arrived = lax.all_to_all(outgoing, "exp", split_axis=0, concat_axis=0, tiled=True)
    hidden_local = w_gate_up.shape[2]
    gate_up = w_gate_up[0].reshape(2 * hidden_local, feature_width)
    row_piece = lax.all_gather(arrived[None], "ctx", axis=0, tiled=True)
    piece_count = row_piece.shape[0]
    rows_flat = row_piece.reshape(-1, feature_width)
    both_parts = lax.dot_general(
        rows_flat, gate_up, (((1,), (1,)), ((), ())), preferred_element_type=jnp.float32
    )
    activation = (jax.nn.silu(both_parts[:, :hidden_local]) * both_parts[:, hidden_local:]).astype(
        jnp.bfloat16
    )
    hidden = activation.reshape(piece_count, expert_count, CAP, hidden_local)
    down_cols = w_down[0]
    column_width = down_cols.shape[1]
    hidden_piece = lax.all_gather(hidden, "ctx", axis=3, tiled=True)
    unit_count = hidden_piece.shape[3]
    made_cols = jnp.dot(
        hidden_piece.reshape(-1, unit_count), down_cols, preferred_element_type=jnp.float32
    )
    made_cols = made_cols.astype(jnp.bfloat16).reshape(ctx_count, expert_count, CAP, column_width)
    returned = lax.all_to_all(
        lax.all_to_all(made_cols, "ctx", split_axis=0, concat_axis=3, tiled=True),
        "exp",
        split_axis=1,
        concat_axis=0,
        tiled=True,
    )
    returned = returned.reshape(expert_count * CAP, feature_width)
    picked = lax.dot_general(
        chooser, returned, (((0,), (0,)), ((), ())), preferred_element_type=jnp.float32
    )
    layer_out = (flat_attended + combine[0][:, None] * picked).astype(jnp.bfloat16)
    return layer_out[None]


def solution(mesh):
    placed = (
        P("exp", "ctx", None),
        P("exp", None, "ctx", None),
        P("exp", "ctx"),
        P("exp", "ctx"),
        P("exp", "ctx"),
        P("exp", None, "ctx", None),
        P("exp", None, "ctx"),
    )
    return jax.shard_map(
        shards, mesh=mesh, in_specs=placed, out_specs=P("exp", "ctx", None), check_vma=False
    )
```

profile of v0, /device:TPU:33, one launch (start us, length us, event | category | flops | bytes accessed | tf_op | source)
XLA Modules:
  0.0 687.9 jit_solution(2477227029983482087)
XLA Ops:
  10.8 2.3 copy.43
  14.7 200.1 %while.19 = (s32[]{:T(128)}, f32[2,16,128]{2,1,0:T(8,128)S(1)}, f32[2,16,128]{2,1,0:T(8,128)S(1)}, f32[2,16,128,128]{3,2,1,0:T(8,128)}, bf16[1,2,128,256]{2,3,1,...) while((s32[]{:T(128)}, f32[2,16,128]{2,1,0:T(8,128)S(1)}, ...), condition=%wide.region_3.4_spmd.clone, body=%wide.region_0.3_spmd.clone.sunk | while | flops 276860928 | bytes 29823224 | solution.py:66
  14.7 4.1 collective-permute-start.1
  18.8 1.9 collective-permute-start
  25.4 3.9 collective-permute-start.1
  29.3 1.9 collective-permute-start
  35.8 5.1 collective-permute-start.1
  41.0 1.9 collective-permute-start
  47.5 3.9 collective-permute-start.1
  51.5 1.9 collective-permute-start
  58.0 3.9 collective-permute-start.1
  62.0 1.9 collective-permute-start
  68.5 3.9 collective-permute-start.1
  72.5 1.9 collective-permute-start
  79.1 2.2 collective-permute-done
  81.3 2.4 collective-permute-start.1
  83.8 1.9 collective-permute-start
  90.3 3.7 collective-permute-done.1
  94.0 2.2 collective-permute-done
  96.1 2.4 collective-permute-start.1
  98.6 1.9 collective-permute-start
  105.1 3.7 collective-permute-done.1
  108.8 2.2 collective-permute-done
  111.0 2.4 collective-permute-start.1
  113.4 1.9 collective-permute-start
  119.9 3.7 collective-permute-done.1
  123.6 2.2 collective-permute-done
  125.8 2.4 collective-permute-start.1
  128.3 1.9 collective-permute-start
  134.8 3.7 collective-permute-done.1
  138.5 2.2 collective-permute-done
  140.6 2.4 collective-permute-start.1
  143.1 1.9 collective-permute-start
  149.6 3.7 collective-permute-done.1
  153.3 2.2 collective-permute-done
  155.5 2.4 collective-permute-start.1
  164.4 3.7 collective-permute-done.1
  168.1 2.2 collective-permute-done
  170.3 2.4 collective-permute-start.1
  172.8 1.9 collective-permute-start
  179.2 3.7 collective-permute-done.1
  182.9 2.2 collective-permute-done
  185.1 2.4 collective-permute-start.1
  187.6 1.9 collective-permute-start
  194.1 3.7 collective-permute-done.1
  197.8 2.2 collective-permute-done
  199.9 2.4 collective-permute-start.1
  202.4 1.9 collective-permute-start
  208.9 3.7 collective-permute-done.1
  212.6 2.2 collective-permute-done
  214.8 3.0 copy.48
  222.5 32.7 %all_to_all.32 = bf16[32,2,4096]{2,1,0:T(2,128)(2,1)} all-to-all(bf16[32,2,4096]{2,1,0:T(2,128)(2,1)S(1)} %reshape.55), channel_id=1, replica_groups=mesh['ctx'=16,'exp'=32] {'exp'}, dimensions={0} | all-to-all | bytes 1048576 | tf_op jit(solution)/shard_map/all_to_all | solution.py:88
  255.5 125.6 %all-gather.6.cloned.1.call-done = bf16[512,2,4096]{2,1,0:T(2,128)(2,1)} async-done(((bf16[32,2,4096]{2,1,0:T(2,128)(2,1)}), bf16[512,2,4096]{2,1,0:T(2,128)(2,1)}) %all-gather.6.cloned.1.call-update) | async-done | bytes 8388624 | tf_op jit(solution)/shard_map/all_gather | solution.py:91
  381.1 13.1 %reshape.56 = bf16[1024,4096]{1,0:T(8,128)(2,1)} reshape(bf16[512,2,4096]{2,1,0:T(2,128)(2,1)} %all-gather.6.cloned.1.call-done) | data formatting | bytes 16777216 | tf_op jit(solution)/shard_map/reshape | solution.py:93
  394.2 6.3 fusion.39
  402.2 149.4 %all-gather.4.cloned.1.call-done = bf16[16,32,2,1536]{1,0,2,3:T(8,128)(2,1)} async-done(((bf16[16,32,2,96]{1,0,2,3:T(8,128)(2,1)}), bf16[16,32,2,1536]{1,0,2,3:T(8,128)(2,1)}) %all-gather.4.cloned.1.call-update) | async-done | bytes 3145744 | tf_op jit(solution)/shard_map/all_gather | solution.py:103
  551.6 20.2 %copy.52 = bf16[16,32,2,1536]{3,2,1,0:T(2,128)(2,1)} copy(bf16[16,32,2,1536]{1,0,2,3:T(8,128)(2,1)} %all-gather.4.cloned.1.call-done) | data formatting | bytes 6291456 | tf_op jit(solution)/shard_map/all_gather | solution.py:103
  571.8 7.5 %reshape.58 = bf16[1024,1536]{1,0:T(8,128)(2,1)} reshape(bf16[16,32,2,1536]{3,2,1,0:T(2,128)(2,1)} %copy.52) | data formatting | bytes 6291456 | tf_op jit(solution)/shard_map/reshape | solution.py:106
  579.3 3.1 convolution_convert_fusion.1
  582.7 43.1 %all_to_all.33 = bf16[16,32,2,256]{3,1,2,0:T(8,128)(2,1)S(1)} all-to-all(bf16[16,32,2,256]{3,1,2,0:T(8,128)(2,1)S(1)} %copy.53), channel_id=1, replica_groups=mesh['ctx'=16,'exp'=32] {'ctx'}, dimensions={0} | all-to-all | bytes 1048576 | tf_op jit(solution)/shard_map/all_to_all | solution.py:110
  627.0 14.2 %all-to-all-start.2 = ((bf16[1,32,2,4096]{3,2,0,1:T(2,128)(2,1)}), bf16[1,32,2,4096]{3,2,0,1:T(2,128)(2,1)S(1)}, u32[]{:S(2)}, u32[]{:S(2)}) async-start(bf16[1,32,2,4096]{3,2,0,1:T(2,128)(2,1)} %reshape.68), calls=%async_computation.2 | async-start | bytes 1048576 | tf_op jit(solution)/shard_map/all_to_all | solution.py:109
  641.3 2.9 copy.56
  644.2 33.6 %all-to-all-done.2 = bf16[1,32,2,4096]{3,2,0,1:T(2,128)(2,1)S(1)} async-done(((bf16[1,32,2,4096]{3,2,0,1:T(2,128)(2,1)}), bf16[1,32,2,4096]{3,2,0,1:T(2,128)(2,1)S(1)}, u32[]{:S(2)}, u32[]{:S(2)}) %all-to-all-start.2) | async-done | bytes 524320 | tf_op jit(solution)/shard_map/all_to_all | solution.py:109
  678.0 3.0 fusion.16
  (266 shorter events, 84.0 us)
Async XLA Ops:
  6.5 387.6 %copy-start = (bf16[1,2,96,4096]{3,2,1,0:T(8,128)(2,1)S(1)}, bf16[1,2,96,4096]{3,2,1,0:T(8,128)(2,1)}, u32[]{:S(2)}) copy-start(bf16[1,2,96,4096]{3,2,1,0:T(8,128)(2,1)} %param.14) | copy-start | bytes 4718596
  6.5 374.5 %all-gather.6.cloned.1.call-start = ((), (), s32[]{:S(2)}) async-start(), calls=%async_computation.4 | async-start | bytes 8912896 | tf_op jit(solution)/shard_map/all_gather | solution.py:91
  10.8 3.9 copy-start.6
  14.7 10.6 %collective-permute-start.1 = (s32[1,1,128]{2,1,0:T(1,128)S(1)}, s32[1,1,128]{2,1,0:T(1,128)S(1)}, u32[]{:S(2)}, u32[]{:S(2)}) collective-permute-start(s32[1,1,128]{2,1,0:T(1,128)S(1)} %copy.83), channel_id=1, source_target_pairs={{0,32},{32,64},{64,96},{96,128},{128,160},{160,192},{192,224},{224... | collective-permute-start | bytes 1544 | tf_op jit(solution)/shard_map/while/body/eval_jaxpr/ppermute | solution.py:16
  18.8 6.5 collective-permute-start
  20.9 1.6 copy-start.1
  25.4 10.5 %collective-permute-start.1 = (s32[1,1,128]{2,1,0:T(1,128)S(1)}, s32[1,1,128]{2,1,0:T(1,128)S(1)}, u32[]{:S(2)}, u32[]{:S(2)}) collective-permute-start(s32[1,1,128]{2,1,0:T(1,128)S(1)} %copy.83), channel_id=1, source_target_pairs={{0,32},{32,64},{64,96},{96,128},{128,160},{160,192},{192,224},{224... | collective-permute-start | bytes 1544 | tf_op jit(solution)/shard_map/while/body/eval_jaxpr/ppermute | solution.py:16
  29.3 6.5 collective-permute-start
  31.4 1.6 copy-start.1
  34.5 1.3 copy-start.2
  35.8 11.7 %collective-permute-start.1 = (s32[1,1,128]{2,1,0:T(1,128)S(1)}, s32[1,1,128]{2,1,0:T(1,128)S(1)}, u32[]{:S(2)}, u32[]{:S(2)}) collective-permute-start(s32[1,1,128]{2,1,0:T(1,128)S(1)} %copy.83), channel_id=1, source_target_pairs={{0,32},{32,64},{64,96},{96,128},{128,160},{160,192},{192,224},{224... | collective-permute-start | bytes 1544 | tf_op jit(solution)/shard_map/while/body/eval_jaxpr/ppermute | solution.py:16
  41.0 6.5 collective-permute-start
  43.0 1.6 copy-start.1
  46.2 1.3 copy-start.2
  47.5 10.5 %collective-permute-start.1 = (s32[1,1,128]{2,1,0:T(1,128)S(1)}, s32[1,1,128]{2,1,0:T(1,128)S(1)}, u32[]{:S(2)}, u32[]{:S(2)}) collective-permute-start(s32[1,1,128]{2,1,0:T(1,128)S(1)} %copy.83), channel_id=1, source_target_pairs={{0,32},{32,64},{64,96},{96,128},{128,160},{160,192},{192,224},{224... | collective-permute-start | bytes 1544 | tf_op jit(solution)/shard_map/while/body/eval_jaxpr/ppermute | solution.py:16
  51.5 6.5 collective-permute-start
  53.5 1.6 copy-start.1
  56.6 1.3 copy-start.2
  58.0 10.5 %collective-permute-start.1 = (s32[1,1,128]{2,1,0:T(1,128)S(1)}, s32[1,1,128]{2,1,0:T(1,128)S(1)}, u32[]{:S(2)}, u32[]{:S(2)}) collective-permute-start(s32[1,1,128]{2,1,0:T(1,128)S(1)} %copy.83), channel_id=1, source_target_pairs={{0,32},{32,64},{64,96},{96,128},{128,160},{160,192},{192,224},{224... | collective-permute-start | bytes 1544 | tf_op jit(solution)/shard_map/while/body/eval_jaxpr/ppermute | solution.py:16
  62.0 6.5 collective-permute-start
  64.0 1.6 copy-start.1
  68.5 10.6 %collective-permute-start.1 = (s32[1,1,128]{2,1,0:T(1,128)S(1)}, s32[1,1,128]{2,1,0:T(1,128)S(1)}, u32[]{:S(2)}, u32[]{:S(2)}) collective-permute-start(s32[1,1,128]{2,1,0:T(1,128)S(1)} %copy.83), channel_id=1, source_target_pairs={{0,32},{32,64},{64,96},{96,128},{128,160},{160,192},{192,224},{224... | collective-permute-start | bytes 1544 | tf_op jit(solution)/shard_map/while/body/eval_jaxpr/ppermute | solution.py:16
  72.5 8.9 %collective-permute-start = (bf16[1,2,128,256]{2,3,1,0:T(8,128)(2,1)S(1)}, bf16[1,2,128,256]{2,3,1,0:T(8,128)(2,1)S(1)}, u32[]{:S(2)}, u32[]{:S(2)}) collective-permute-start(bf16[1,2,128,256]{2,3,1,0:T(8,128)(2,1)S(1)} %copy.82), channel_id=1, source_target_pairs={{0,32},{32,64},{64,96},{96,128},{128,160},{160,192},{192,224},{224... | collective-permute-start | bytes 393224 | tf_op jit(solution)/shard_map/while/body/eval_jaxpr/ppermute | solution.py:16
  74.5 1.6 copy-start.1
  77.6 1.3 copy-start.2
  81.3 12.7 %collective-permute-start.1 = (s32[1,1,128]{2,1,0:T(1,128)S(1)}, s32[1,1,128]{2,1,0:T(1,128)S(1)}, u32[]{:S(2)}, u32[]{:S(2)}) collective-permute-start(s32[1,1,128]{2,1,0:T(1,128)S(1)} %copy.83), channel_id=1, source_target_pairs={{0,32},{32,64},{64,96},{96,128},{128,160},{160,192},{192,224},{224... | collective-permute-start | bytes 1544 | tf_op jit(solution)/shard_map/while/body/eval_jaxpr/ppermute | solution.py:16
  83.8 12.4 %collective-permute-start = (bf16[1,2,128,256]{2,3,1,0:T(8,128)(2,1)S(1)}, bf16[1,2,128,256]{2,3,1,0:T(8,128)(2,1)S(1)}, u32[]{:S(2)}, u32[]{:S(2)}) collective-permute-start(bf16[1,2,128,256]{2,3,1,0:T(8,128)(2,1)S(1)} %copy.82), channel_id=1, source_target_pairs={{0,32},{32,64},{64,96},{96,128},{128,160},{160,192},{192,224},{224... | collective-permute-start | bytes 393224 | tf_op jit(solution)/shard_map/while/body/eval_jaxpr/ppermute | solution.py:16
  85.8 1.6 copy-start.1
  88.9 1.3 copy-start.2
  96.1 12.7 %collective-permute-start.1 = (s32[1,1,128]{2,1,0:T(1,128)S(1)}, s32[1,1,128]{2,1,0:T(1,128)S(1)}, u32[]{:S(2)}, u32[]{:S(2)}) collective-permute-start(s32[1,1,128]{2,1,0:T(1,128)S(1)} %copy.83), channel_id=1, source_target_pairs={{0,32},{32,64},{64,96},{96,128},{128,160},{160,192},{192,224},{224... | collective-permute-start | bytes 1544 | tf_op jit(solution)/shard_map/while/body/eval_jaxpr/ppermute | solution.py:16
  98.6 12.4 %collective-permute-start = (bf16[1,2,128,256]{2,3,1,0:T(8,128)(2,1)S(1)}, bf16[1,2,128,256]{2,3,1,0:T(8,128)(2,1)S(1)}, u32[]{:S(2)}, u32[]{:S(2)}) collective-permute-start(bf16[1,2,128,256]{2,3,1,0:T(8,128)(2,1)S(1)} %copy.82), channel_id=1, source_target_pairs={{0,32},{32,64},{64,96},{96,128},{128,160},{160,192},{192,224},{224... | collective-permute-start | bytes 393224 | tf_op jit(solution)/shard_map/while/body/eval_jaxpr/ppermute | solution.py:16
  100.7 1.6 copy-start.1
  103.8 1.3 copy-start.2
  111.0 12.7 %collective-permute-start.1 = (s32[1,1,128]{2,1,0:T(1,128)S(1)}, s32[1,1,128]{2,1,0:T(1,128)S(1)}, u32[]{:S(2)}, u32[]{:S(2)}) collective-permute-start(s32[1,1,128]{2,1,0:T(1,128)S(1)} %copy.83), channel_id=1, source_target_pairs={{0,32},{32,64},{64,96},{96,128},{128,160},{160,192},{192,224},{224... | collective-permute-start | bytes 1544 | tf_op jit(solution)/shard_map/while/body/eval_jaxpr/ppermute | solution.py:16
  113.4 12.4 %collective-permute-start = (bf16[1,2,128,256]{2,3,1,0:T(8,128)(2,1)S(1)}, bf16[1,2,128,256]{2,3,1,0:T(8,128)(2,1)S(1)}, u32[]{:S(2)}, u32[]{:S(2)}) collective-permute-start(bf16[1,2,128,256]{2,3,1,0:T(8,128)(2,1)S(1)} %copy.82), channel_id=1, source_target_pairs={{0,32},{32,64},{64,96},{96,128},{128,160},{160,192},{192,224},{224... | collective-permute-start | bytes 393224 | tf_op jit(solution)/shard_map/while/body/eval_jaxpr/ppermute | solution.py:16
  115.5 1.6 copy-start.1
  118.6 1.3 copy-start.2
  125.8 12.7 %collective-permute-start.1 = (s32[1,1,128]{2,1,0:T(1,128)S(1)}, s32[1,1,128]{2,1,0:T(1,128)S(1)}, u32[]{:S(2)}, u32[]{:S(2)}) collective-permute-start(s32[1,1,128]{2,1,0:T(1,128)S(1)} %copy.83), channel_id=1, source_target_pairs={{0,32},{32,64},{64,96},{96,128},{128,160},{160,192},{192,224},{224... | collective-permute-start | bytes 1544 | tf_op jit(solution)/shard_map/while/body/eval_jaxpr/ppermute | solution.py:16
  128.3 12.4 %collective-permute-start = (bf16[1,2,128,256]{2,3,1,0:T(8,128)(2,1)S(1)}, bf16[1,2,128,256]{2,3,1,0:T(8,128)(2,1)S(1)}, u32[]{:S(2)}, u32[]{:S(2)}) collective-permute-start(bf16[1,2,128,256]{2,3,1,0:T(8,128)(2,1)S(1)} %copy.82), channel_id=1, source_target_pairs={{0,32},{32,64},{64,96},{96,128},{128,160},{160,192},{192,224},{224... | collective-permute-start | bytes 393224 | tf_op jit(solution)/shard_map/while/body/eval_jaxpr/ppermute | solution.py:16
  130.3 1.6 copy-start.1
  133.4 1.3 copy-start.2
  140.6 12.7 %collective-permute-start.1 = (s32[1,1,128]{2,1,0:T(1,128)S(1)}, s32[1,1,128]{2,1,0:T(1,128)S(1)}, u32[]{:S(2)}, u32[]{:S(2)}) collective-permute-start(s32[1,1,128]{2,1,0:T(1,128)S(1)} %copy.83), channel_id=1, source_target_pairs={{0,32},{32,64},{64,96},{96,128},{128,160},{160,192},{192,224},{224... | collective-permute-start | bytes 1544 | tf_op jit(solution)/shard_map/while/body/eval_jaxpr/ppermute | solution.py:16
  143.1 12.4 %collective-permute-start = (bf16[1,2,128,256]{2,3,1,0:T(8,128)(2,1)S(1)}, bf16[1,2,128,256]{2,3,1,0:T(8,128)(2,1)S(1)}, u32[]{:S(2)}, u32[]{:S(2)}) collective-permute-start(bf16[1,2,128,256]{2,3,1,0:T(8,128)(2,1)S(1)} %copy.82), channel_id=1, source_target_pairs={{0,32},{32,64},{64,96},{96,128},{128,160},{160,192},{192,224},{224... | collective-permute-start | bytes 393224 | tf_op jit(solution)/shard_map/while/body/eval_jaxpr/ppermute | solution.py:16
  145.1 1.6 copy-start.1
  155.5 12.7 %collective-permute-start.1 = (s32[1,1,128]{2,1,0:T(1,128)S(1)}, s32[1,1,128]{2,1,0:T(1,128)S(1)}, u32[]{:S(2)}, u32[]{:S(2)}) collective-permute-start(s32[1,1,128]{2,1,0:T(1,128)S(1)} %copy.83), channel_id=1, source_target_pairs={{0,32},{32,64},{64,96},{96,128},{128,160},{160,192},{192,224},{224... | collective-permute-start | bytes 1544 | tf_op jit(solution)/shard_map/while/body/eval_jaxpr/ppermute | solution.py:16
  157.9 12.4 %collective-permute-start = (bf16[1,2,128,256]{2,3,1,0:T(8,128)(2,1)S(1)}, bf16[1,2,128,256]{2,3,1,0:T(8,128)(2,1)S(1)}, u32[]{:S(2)}, u32[]{:S(2)}) collective-permute-start(bf16[1,2,128,256]{2,3,1,0:T(8,128)(2,1)S(1)} %copy.82), channel_id=1, source_target_pairs={{0,32},{32,64},{64,96},{96,128},{128,160},{160,192},{192,224},{224... | collective-permute-start | bytes 393224 | tf_op jit(solution)/shard_map/while/body/eval_jaxpr/ppermute | solution.py:16
  160.0 1.6 copy-start.1
  163.1 1.3 copy-start.2
  170.3 12.7 %collective-permute-start.1 = (s32[1,1,128]{2,1,0:T(1,128)S(1)}, s32[1,1,128]{2,1,0:T(1,128)S(1)}, u32[]{:S(2)}, u32[]{:S(2)}) collective-permute-start(s32[1,1,128]{2,1,0:T(1,128)S(1)} %copy.83), channel_id=1, source_target_pairs={{0,32},{32,64},{64,96},{96,128},{128,160},{160,192},{192,224},{224... | collective-permute-start | bytes 1544 | tf_op jit(solution)/shard_map/while/body/eval_jaxpr/ppermute | solution.py:16
  172.8 12.4 %collective-permute-start = (bf16[1,2,128,256]{2,3,1,0:T(8,128)(2,1)S(1)}, bf16[1,2,128,256]{2,3,1,0:T(8,128)(2,1)S(1)}, u32[]{:S(2)}, u32[]{:S(2)}) collective-permute-start(bf16[1,2,128,256]{2,3,1,0:T(8,128)(2,1)S(1)} %copy.82), channel_id=1, source_target_pairs={{0,32},{32,64},{64,96},{96,128},{128,160},{160,192},{192,224},{224... | collective-permute-start | bytes 393224 | tf_op jit(solution)/shard_map/while/body/eval_jaxpr/ppermute | solution.py:16
  174.8 1.6 copy-start.1
  177.9 1.3 copy-start.2
  185.1 12.7 %collective-permute-start.1 = (s32[1,1,128]{2,1,0:T(1,128)S(1)}, s32[1,1,128]{2,1,0:T(1,128)S(1)}, u32[]{:S(2)}, u32[]{:S(2)}) collective-permute-start(s32[1,1,128]{2,1,0:T(1,128)S(1)} %copy.83), channel_id=1, source_target_pairs={{0,32},{32,64},{64,96},{96,128},{128,160},{160,192},{192,224},{224... | collective-permute-start | bytes 1544 | tf_op jit(solution)/shard_map/while/body/eval_jaxpr/ppermute | solution.py:16
  187.6 12.4 %collective-permute-start = (bf16[1,2,128,256]{2,3,1,0:T(8,128)(2,1)S(1)}, bf16[1,2,128,256]{2,3,1,0:T(8,128)(2,1)S(1)}, u32[]{:S(2)}, u32[]{:S(2)}) collective-permute-start(bf16[1,2,128,256]{2,3,1,0:T(8,128)(2,1)S(1)} %copy.82), channel_id=1, source_target_pairs={{0,32},{32,64},{64,96},{96,128},{128,160},{160,192},{192,224},{224... | collective-permute-start | bytes 393224 | tf_op jit(solution)/shard_map/while/body/eval_jaxpr/ppermute | solution.py:16
  189.6 1.6 copy-start.1
  199.9 12.7 %collective-permute-start.1 = (s32[1,1,128]{2,1,0:T(1,128)S(1)}, s32[1,1,128]{2,1,0:T(1,128)S(1)}, u32[]{:S(2)}, u32[]{:S(2)}) collective-permute-start(s32[1,1,128]{2,1,0:T(1,128)S(1)} %copy.83), channel_id=1, source_target_pairs={{0,32},{32,64},{64,96},{96,128},{128,160},{160,192},{192,224},{224... | collective-permute-start | bytes 1544 | tf_op jit(solution)/shard_map/while/body/eval_jaxpr/ppermute | solution.py:16
  202.4 12.4 %collective-permute-start = (bf16[1,2,128,256]{2,3,1,0:T(8,128)(2,1)S(1)}, bf16[1,2,128,256]{2,3,1,0:T(8,128)(2,1)S(1)}, u32[]{:S(2)}, u32[]{:S(2)}) collective-permute-start(bf16[1,2,128,256]{2,3,1,0:T(8,128)(2,1)S(1)} %copy.82), channel_id=1, source_target_pairs={{0,32},{32,64},{64,96},{96,128},{128,160},{160,192},{192,224},{224... | collective-permute-start | bytes 393224 | tf_op jit(solution)/shard_map/while/body/eval_jaxpr/ppermute | solution.py:16
  204.5 1.6 copy-start.1
  214.8 3.1 copy-start.3
  217.9 1.6 copy-start.5
  220.3 1.3 copy-start.4
  255.3 296.3 %all-gather.4.cloned.1.call-start = ((), (), s32[]{:S(2)}) async-start(), calls=%async_computation.3 | async-start | bytes 13369344 | tf_op jit(solution)/shard_map/all_gather | solution.py:103
  627.0 50.7 %all-to-all-start.2 = ((bf16[1,32,2,4096]{3,2,0,1:T(2,128)(2,1)}), bf16[1,32,2,4096]{3,2,0,1:T(2,128)(2,1)S(1)}, u32[]{:S(2)}, u32[]{:S(2)}) async-start(bf16[1,32,2,4096]{3,2,0,1:T(2,128)(2,1)} %reshape.68), calls=%async_computation.2 | async-start | bytes 1048576 | tf_op jit(solution)/shard_map/all_to_all | solution.py:109
  641.3 36.7 %copy-start.7 = (f32[1,128]{1,0:T(1,128)S(1)}, f32[1,128]{1,0:T(1,128)}, u32[]{:S(2)}) copy-start(f32[1,128]{1,0:T(1,128)} %param.13) | copy-start | bytes 1540
  (5 other events, 6.7 us)
Sparse Core Ops, SparseCore 0:
  255.4 125.6 all-gather.5
  402.3 149.2 all-gather.3
where the time goes:
time: 691 us; the launch traced here: 688 us
  waiting for transfers between devices  364 us (53%)
  starting transfers between devices  90.1 us (13%)
  local copies, waits for them, and re-layouts  85.2 us (12%)
  blocking collectives  75.9 us (11%)
  matrix products  44.7 us (6%)
  between operations  13.6 us (2%)
  other arithmetic  13.1 us (2%)
    all_gather x1, waiting for transfers between devices, shards(): hidden_piece = lax.all_gather(hidden, 'ctx', axis=3, tiled=True)  149 us
    all_gather x1, waiting for transfers between devices, shards(): row_piece = lax.all_gather(arrived[None], 'ctx', axis=0, tiled=True)  126 us
    ppermute x30, starting transfers between devices, shifted(): lax.ppermute(value, axis, [(i, (i + by) % length) for i in range(length)])  75.7 us
    ppermute x30, waiting for transfers between devices, shifted(): lax.ppermute(value, axis, [(i, (i + by) % length) for i in range(length)])  55.2 us
    all_to_all x1, blocking collectives, shards(): lax.all_to_all(made_cols, 'ctx', split_axis=0, concat_axis=3, tiled=True)  43.1 us
    all_to_all x1, waiting for transfers between devices, shards(): lax.all_to_all(lax.all_to_all(made_cols, 'ctx', split_axis=0, concat_axis...  33.6 us
    all_to_all x1, blocking collectives, shards(): lax.all_to_all(outgoing, 'exp', split_axis=0, concat_axis=0, tiled=True)  32.7 us
    while x105, local copies, waits for them, and re-layouts  27.2 us
  transfers between devices with their start and end apart: 33, of which 23 were waited for; matrix products, arithmetic and copies ran while one was open for 6% of the time, Pallas kernels for 0%

commit v1 on v0

v1 whole, which is shorter than its diff:
```python
import functools

import jax
import jax.numpy as jnp
from jax import lax
from jax.experimental import pallas as pl
from jax.experimental.pallas import tpu as pltpu
from jax.sharding import PartitionSpec as P

HD = 128
CAP = 2
EPS = 1e-06
LOWEST = -1e30
LOG2E = 1.4426950408889634
REACH = 1024

BF = jnp.bfloat16
F32 = jnp.float32
MESH = pl.DeviceIdType.MESH
NT = (((1,), (1,)), ((), ()))
TN = (((0,), (0,)), ((), ()))


def remote(src, dst, send_sem, recv_sem, target):
    return pltpu.make_async_remote_copy(
        src_ref=src,
        dst_ref=dst,
        send_sem=send_sem,
        recv_sem=recv_sem,
        device_id=target,
        device_id_type=MESH,
    )


def spread_kernel(
    nctx, kv_ref, doc_ref, kv_out, doc_out, got, got_doc, sent, sent_doc, shown, shown_doc
):
    tok = kv_ref.shape[1]
    seg = nctx // 2
    reach = min(seg - 1, -(-REACH // (2 * tok)))
    ctx = lax.axis_index("ctx")
    exp = lax.axis_index("exp")
    core = lax.rem(ctx, 2)
    pos = ctx // 2
    sibling = (ctx + 1 - 2 * core, exp)

    def block(b):
        return pl.ds(pl.multiple_of(b * tok, tok), tok)

    def neighbour(way):
        return (ctx + 2 * way, exp)

    def has(p):
        return jnp.logical_and(p >= 0, p < seg)

    barrier = pltpu.get_barrier_semaphore()
    pl.semaphore_signal(barrier, inc=1, device_id=sibling, device_id_type=MESH)
    for way in (1, -1):

        @pl.when(has(pos + way))
        def _():
            pl.semaphore_signal(barrier, inc=1, device_id=neighbour(way), device_id_type=MESH)

    pl.semaphore_wait(
        barrier, 1 + (pos > 0).astype(jnp.int32) + (pos < seg - 1).astype(jnp.int32)
    )

    def moves(b, sems, doc_sem, target, first):
        out = []
        for part in range(2):
            src = kv_ref.at[part] if first else kv_out.at[part, block(b)]
            out.append(
                remote(src, kv_out.at[part, block(b)], sems.at[part], got.at[b, part], target)
            )
        src = doc_ref if first else doc_out.at[b]
        out.append(remote(src, doc_out.at[b], doc_sem, got_doc.at[b], target))
        return out

    def along(way, t, b):
        d = 0 if way == 1 else 1
        return moves(b, sent.at[d, t], sent_doc.at[d, t], neighbour(way), t == 0)

    def across(b, first):
        return moves(b, shown.at[b], shown_doc.at[b], sibling, first)

    for way in (1, -1):

        @pl.when(has(pos + way))
        def _():
            for copy in along(way, 0, ctx):
                copy.start()

    for copy in across(ctx, True):
        copy.start()
    kv_out[:, block(ctx), :] = kv_ref[...]
    doc_out[ctx] = doc_ref[...]

    for t in range(1, reach + 1):
        for way in (1, -1):
            source = pos - way * t
            b = 2 * source + core

            @pl.when(has(source))
            def _():
                there = across(b, False)
                on = along(way, t, b) if t < reach else None
                for n in range(3):
                    there[n].wait_recv()
                    if on is not None:

                        @pl.when(has(pos + way))
                        def _():
                            on[n].start()

                    there[n].start()

    for t in range(0, reach + 1):
        for way in (1, -1):
            source = pos - way * t
            b = 2 * source + core

            @pl.when(has(source))
            def _():
                if t > 0 or way == 1:
                    for copy in across(2 * source + 1 - core, False):
                        copy.wait_recv()
                    for copy in across(b, False):
                        copy.wait_send()
                if t < reach:

                    @pl.when(has(pos + way))
                    def _():
                        for copy in along(way, t, b):
                            copy.wait_send()


def spread(kv, doc, nctx):
    _, tok, width = kv.shape
    return pl.pallas_call(
        functools.partial(spread_kernel, nctx),
        out_shape=(
            jax.ShapeDtypeStruct((2, nctx * tok, width), BF),
            jax.ShapeDtypeStruct((nctx, 8, tok), jnp.int32),
        ),
        in_specs=[pl.BlockSpec(memory_space=pltpu.VMEM)] * 2,
        out_specs=(pl.BlockSpec(memory_space=pltpu.VMEM),) * 2,
        scratch_shapes=[
            pltpu.SemaphoreType.DMA((nctx, 2)),
            pltpu.SemaphoreType.DMA((nctx,)),
            pltpu.SemaphoreType.DMA((2, 8, 2)),
            pltpu.SemaphoreType.DMA((2, 8)),
            pltpu.SemaphoreType.DMA((nctx, 2)),
            pltpu.SemaphoreType.DMA((nctx,)),
        ],
        compiler_params=pltpu.CompilerParams(
            collective_id=0, has_side_effects=True, vmem_limit_bytes=16 << 20
        ),
    )(kv, doc)


def wanted_slot(r, columns):
    d, i = r // 16, lax.rem(r, 4)
    return (columns * (i // 2) + d) * CAP + lax.rem(i, 2)


def quarter_of(r):
    return lax.rem(r, 16) // 4


def slots(ids, earlier, experts):
    kept = jnp.logical_and(ids < experts, earlier < CAP)
    return jnp.where(kept, ids * CAP + earlier, -1)


def attend_kernel(
    experts, kv_ref, doc_ref, q_ref, qdoc_ref, idr_ref, idc_ref, att_ref, send_ref, s_scr, m_scr, l_scr, a_scr
):
    tok, width = q_ref.shape
    nctx = doc_ref.shape[0]
    groups = kv_ref.shape[2] // HD
    per = width // HD // groups
    step = 2 * tok
    seg = nctx // 2
    reach = min(seg - 1, -(-REACH // step))
    pos = lax.axis_index("ctx") // 2
    scale = HD ** (-0.5) * LOG2E

    where = lax.broadcasted_iota(jnp.int32, (nctx, 8, tok), 0) // 2
    docs = jnp.where(where < pos - reach, -1, jnp.where(where > pos + reach, 1 << 20, doc_ref[...]))
    qdoc = qdoc_ref[...]
    low = jnp.min(qdoc)
    high = jnp.max(qdoc)
    begin = jnp.sum((docs < low).astype(jnp.int32)) // 8
    end = jnp.sum((docs <= high).astype(jnp.int32)) // 8
    first = begin // step
    last = (end + step - 1) // step

    squares = jnp.zeros((tok, HD), F32)
    for g in range(groups):
        lanes = slice(g * HD, (g + 1) * HD)
        m_scr[...] = jnp.full(m_scr.shape, LOWEST, F32)
        l_scr[...] = jnp.zeros(l_scr.shape, F32)
        a_scr[...] = jnp.zeros(a_scr.shape, F32)

        @pl.loop(first, last)
        def _(kb):
            keys = kv_ref[0, pl.ds(pl.multiple_of(kb * step, step), step), lanes]
            kdoc = jnp.concatenate([doc_ref[2 * kb, 0:1], doc_ref[2 * kb + 1, 0:1]], axis=1)
            bias = jnp.where(kdoc == qdoc, 0.0, LOWEST).astype(F32)
            for h in range(per):
                at = slice((g * per + h) * HD, (g * per + h + 1) * HD)
                rows = slice(h * tok, (h + 1) * tok)
                s = lax.dot_general(q_ref[:, at], keys, NT, preferred_element_type=F32) + bias
                s_scr[kb, rows] = s
                m_scr[rows] = jnp.maximum(
                    m_scr[rows], jnp.maximum(s[:, :HD], s[:, HD:])
                )

        for h in range(per):
            rows = slice(h * tok, (h + 1) * tok)
            m_scr[rows] = jnp.broadcast_to(
                jnp.max(m_scr[rows], axis=1, keepdims=True), (tok, HD)
            )

        @pl.loop(first, last)
        def _(kb):
            values = kv_ref[1, pl.ds(pl.multiple_of(kb * step, step), step), lanes]
            for h in range(per):
                rows = slice(h * tok, (h + 1) * tok)
                top = m_scr[rows]
                s = s_scr[kb, rows]
                p = jnp.exp2((s - jnp.concatenate([top, top], axis=1)) * scale)
                l_scr[rows] = l_scr[rows] + (p[:, :HD] + p[:, HD:])
                a_scr[rows] = a_scr[rows] + jnp.dot(
                    p.astype(BF), values, preferred_element_type=F32
                )

        for h in range(per):
            at = slice((g * per + h) * HD, (g * per + h + 1) * HD)
            rows = slice(h * tok, (h + 1) * tok)
            total = jnp.sum(l_scr[rows], axis=1, keepdims=True)
            mixed = (a_scr[rows] / total).astype(BF)
            att_ref[:, at] = mixed
            wide = mixed.astype(F32)
            squares = squares + wide * wide

    inverse = lax.rsqrt(jnp.sum(squares, axis=1, keepdims=True) / width + EPS)
    idr = idr_ref[0:1]
    idc = idc_ref[...]
    before = lax.broadcasted_iota(jnp.int32, (tok, tok), 0) < lax.broadcasted_iota(
        jnp.int32, (tok, tok), 1
    )
    earlier = jnp.sum(
        jnp.where(jnp.logical_and(before, idc == idr), 1, 0), axis=0, keepdims=True
    )
    slot = slots(idr, earlier, experts)
    count = send_ref.shape[0]
    r = lax.broadcasted_iota(jnp.int32, (count, tok), 0)
    match = wanted_slot(r, count // 16) == slot
    part = quarter_of(r)
    span = width // 4
    for piece in range(0, span, 256):
        total = jnp.zeros((count, 256), F32)
        for q in range(4):
            chooser = jnp.where(jnp.logical_and(match, part == q), 1.0, 0.0).astype(BF)
            att = att_ref[:, q * span + piece : q * span + piece + 256].astype(F32)
            normed = (att * inverse).astype(BF)
            total = total + jnp.dot(chooser, normed, preferred_element_type=F32)
        send_ref[:, piece : piece + 256] = total.astype(BF)


def attend(kv, doc, q, qdoc, idr, idc, experts):
    tok, width = q.shape
    nctx = doc.shape[0]
    per = width // HD // (kv.shape[2] // HD)
    count = 16 * (experts // 2)
    vm = pl.BlockSpec(memory_space=pltpu.VMEM)
    return pl.pallas_call(
        functools.partial(attend_kernel, experts),
        out_shape=(
            jax.ShapeDtypeStruct((tok, width), BF),
            jax.ShapeDtypeStruct((count, width // 4), BF),
        ),
        in_specs=[vm] * 6,
        out_specs=(vm, vm),
        scratch_shapes=[
            pltpu.VMEM((nctx // 2, per * tok, 2 * tok), F32),
            pltpu.VMEM((per * tok, HD), F32),
            pltpu.VMEM((per * tok, HD), F32),
            pltpu.VMEM((per * tok, HD), F32),
        ],
        compiler_params=pltpu.CompilerParams(vmem_limit_bytes=48 << 20),
    )(kv, doc, q, qdoc, idr, idc)


def experts_kernel(
    nctx, nexp, send_ref, wgu_ref, wd_ref, back_ref,
    came, rows, transit, hid, made, ret, send2, back,
    a_sent, a_got, r_sent, r_got, t_sent, t_got, x_sent, x_got,
    h_sent, h_got, y_sent, y_got, d_sent, d_got, b_sent, b_got,
):
    seg = nctx // 2
    half = seg // 2
    xy = nexp // 2
    span = send_ref.shape[1]
    width = 4 * span
    piece = xy
    units = wgu_ref.shape[0] // 2
    cols = wd_ref.shape[1]
    ctx = lax.axis_index("ctx")
    exp = lax.axis_index("exp")
    core = lax.rem(ctx, 2)
    pos = ctx // 2
    zhi = exp // xy
    place = lax.rem(exp, xy)
    layer = zhi * seg + pos
    layers = 2 * seg
    sibling = (ctx + 1 - 2 * core, exp)

    def at_layer(z, c):
        z = lax.rem(z + 2 * layers, layers)
        return (2 * lax.rem(z, seg) + c, (z // seg) * xy + place)

    def at_place(d):
        return (ctx, zhi * xy + d)

    barrier = pltpu.get_barrier_semaphore()

    @pl.loop(1, xy)
    def _(j):
        pl.semaphore_signal(
            barrier, inc=1, device_id=at_place(lax.rem(place + j, xy)), device_id_type=MESH
        )

    @pl.loop(1, 2 * layers)
    def _(j):
        me = 2 * layer + core
        n = lax.rem(me + j, 2 * layers)
        pl.semaphore_signal(
            barrier, inc=1, device_id=at_layer(n // 2, lax.rem(n, 2)), device_id_type=MESH
        )

    pl.semaphore_wait(barrier, xy - 1 + 2 * layers - 1)

    def block16(d):
        return pl.ds(pl.multiple_of(d * 16, 16), 16)

    def swap(src, dst, sent, got, d):
        out = remote(src.at[block16(d)], dst.at[block16(place)], sent.at[d], got.at[place], at_place(d))
        into = remote(src.at[block16(place)], dst.at[block16(d)], sent.at[place], got.at[d], at_place(d))
        return out, into

    def exchange(src, dst, sent, got):
        @pl.loop(1, xy)
        def _(j):
            swap(src, dst, sent, got, lax.rem(place + j, xy))[0].start()

        dst[block16(place)] = src[block16(place)]

        @pl.loop(1, xy)
        def _(j):
            swap(src, dst, sent, got, lax.rem(place + xy - j, xy))[1].wait_recv()

    def exchange_end(src, dst, sent, got):
        @pl.loop(1, xy)
        def _(j):
            swap(src, dst, sent, got, lax.rem(place + j, xy))[0].wait_send()

    exchange(send_ref, came, a_sent, a_got)
    r = lax.broadcasted_iota(jnp.int32, (2 * xy, 16 * xy), 0)
    c = lax.broadcasted_iota(jnp.int32, (2 * xy, 16 * xy), 1)
    for side in range(2):
        z = zhi if side == 0 else 1 - zhi
        for q in range(4):
            pick = jnp.where(
                c == (r // 2) * 16 + q * 4 + 2 * z + lax.rem(r, 2), 1.0, 0.0
            ).astype(BF)
            got = jnp.dot(pick, came[...], preferred_element_type=F32).astype(BF)
            for h in range(2):
                kept = got[h * piece : (h + 1) * piece]
                if side == 0:
                    rows[layer, core, h, :, q * span : (q + 1) * span] = kept
                else:
                    transit[pos, h, :, q * span : (q + 1) * span] = kept

    def ring(z):
        return lax.rem(z + 2 * layers, layers)

    def rank_of(way):
        return pos if way == 1 else seg - 1 - pos

    def chunk_moves(way, t, h):
        d = 0 if way == 1 else 1
        k = rank_of(way)
        z = ring(layer - way * (t - 1))
        p = lax.rem(pos - way * (t - 1) + 2 * seg, seg)
        target = at_layer(layer + way, core)
        return [
            (
                jnp.logical_and(k < seg - 1, t <= k + 1 - half),
                remote(transit.at[p, h], transit.at[p, h], t_sent.at[d, t, h], t_got.at[p, h], target),
            ),
            (
                jnp.logical_and(k == seg - 1, t <= half),
                remote(transit.at[p, h], rows.at[z, core, h], t_sent.at[d, t, h], r_got.at[z, h], target),
            ),
            (
                jnp.logical_and(k < seg - 1, t <= k + 1 + half),
                remote(rows.at[z, core, h], rows.at[z, core, h], r_sent.at[d, t, h], r_got.at[z, h], target),
            ),
        ]

    def chunk_start(way, t, h):
        for cond, copy in chunk_moves(way, t, h):

            @pl.when(cond)
            def _():
                copy.start()

    def show(z, h, c):
        return remote(rows.at[z, c, h], rows.at[z, c, h], x_sent.at[z, h], x_got.at[z, h], sibling)

    for h in range(2):
        for way in (1, -1):
            chunk_start(way, 1, h)
        show(layer, h, core).start()

    steps = seg - 1 + half

    @pl.loop(1, steps + 1)
    def _(t):
        for h in range(2):
            for way in (1, -1):
                k = rank_of(way)
                z = ring(layer - way * t)
                p = lax.rem(pos - way * t + 2 * seg, seg)

                @pl.when(t <= k - half)
                def _():
                    remote(
                        transit.at[p, h], transit.at[p, h], t_sent.at[0, 0, h], t_got.at[p, h], sibling
                    ).wait_recv()

                @pl.when(t <= k + half)
                def _():
                    remote(
                        rows.at[z, core, h], rows.at[z, core, h], r_sent.at[0, 0, h], r_got.at[z, h], sibling
                    ).wait_recv()

                chunk_start(way, t + 1, h)

                @pl.when(t <= k + half)
                def _():
                    show(z, h, core).start()

    @pl.loop(0, layers)
    def _(z):
        for h in range(2):
            show(z, h, 1 - core).wait_recv()

    def hid_moves(way, t, s):
        d = 0 if way == 1 else 1
        k = rank_of(way)
        b = 2 * (pos - way * (t - 1)) + core
        target = (ctx + 2 * way, exp)
        return (
            jnp.logical_and(k < seg - 1, t <= k + 1),
            remote(hid.at[s, b], hid.at[s, b], h_sent.at[d, t, s], h_got.at[s, b], target),
        )

    def hid_start(way, t, s):
        cond, copy = hid_moves(way, t, s)

        @pl.when(cond)
        def _():
            copy.start()

    def hid_show(s, b):
        return remote(hid.at[s, b], hid.at[s, b], y_sent.at[s, b], y_got.at[s, b], sibling)

    chunk = 4 * xy
    some = seg * chunk
    for s in range(2):
        x = rows[s * seg : (s + 1) * seg].reshape(some, width)
        both = lax.dot_general(wgu_ref[...], x, NT, preferred_element_type=F32)
        gate, upper = both[:units], both[units:]
        hid[s, ctx] = (gate / (1.0 + jnp.exp(-gate)) * upper).astype(BF)
        for way in (1, -1):
            hid_start(way, 1, s)
        hid_show(s, ctx).start()

    @pl.loop(1, seg)
    def _(t):
        for s in range(2):
            for way in (1, -1):
                k = rank_of(way)
                b = 2 * (pos - way * t) + core

                @pl.when(t <= k)
                def _():
                    remote(
                        hid.at[s, b], hid.at[s, b], h_sent.at[0, 0, s], h_got.at[s, b], sibling
                    ).wait_recv()

                hid_start(way, t + 1, s)

                @pl.when(t <= k)
                def _():
                    hid_show(s, b).start()

    fold = nctx // 4

    def home(z, c):
        slot = (lax.rem(ctx, fold), zhi, ctx // fold)
        n = zhi * nctx + ctx
        return remote(
            made.at[z, c], ret.at[slot], d_sent.at[2 * z + c], d_got.at[n], at_layer(z, c)
        )

    def home_from(z, c):
        n_ctx = 2 * lax.rem(z, seg) + c
        n = (z // seg) * nctx + n_ctx
        slot = (lax.rem(n_ctx, fold), z // seg, n_ctx // fold)
        return remote(made.at[z, c], ret.at[slot], d_sent.at[2 * z + c], d_got.at[n], at_layer(z, c))

    for s in range(2):

        @pl.loop(0, seg)
        def _(p):
            hid_show(s, 2 * p + 1 - core).wait_recv()

        hidden = hid[s].reshape(nctx * units, some)
        out = lax.dot_general(hidden, wd_ref[...], TN, preferred_element_type=F32)
        made[s * seg : (s + 1) * seg] = out.astype(BF).reshape(seg, 2, 2 * xy, cols)

        me = 2 * layer + core

        @pl.loop(0, nctx)
        def _(j):
            n = lax.rem(me + j, nctx) + s * nctx

            @pl.when(n != me)
            def _():
                home(n // 2, lax.rem(n, 2)).start()

    ret[lax.rem(ctx, fold), zhi, ctx // fold] = made[layer, core]

    @pl.loop(1, 2 * layers)
    def _(j):
        n = lax.rem(2 * layer + core + j, 2 * layers)
        home_from(n // 2, lax.rem(n, 2)).wait_recv()

    r = lax.broadcasted_iota(jnp.int32, (16 * xy, 16 * xy), 0)
    c = lax.broadcasted_iota(jnp.int32, (16 * xy, 16 * xy), 1)
    i = lax.rem(r, 4)
    place_back = jnp.where(
        c == ((i // 2) * 4 + quarter_of(r)) * 2 * xy + 2 * (r // 16) + lax.rem(i, 2), 1.0, 0.0
    ).astype(BF)
    for m in range(fold):
        got = ret[m].reshape(16 * xy, cols)
        send2[:, m * cols : (m + 1) * cols] = jnp.dot(
            place_back, got, preferred_element_type=F32
        ).astype(BF)
    exchange(send2, back, b_sent, b_got)
    back_ref[...] = back[...]

    exchange_end(send_ref, came, a_sent, a_got)
    exchange_end(send2, back, b_sent, b_got)

    @pl.loop(1, steps + 2)
    def _(t):
        for h in range(2):
            for way in (1, -1):
                for cond, copy in chunk_moves(way, t, h):

                    @pl.when(cond)
                    def _():
                        copy.wait_send()

    @pl.loop(0, layers)
    def _(z):
        for h in range(2):
            show(z, h, core).wait_send()

    @pl.loop(1, seg + 1)
    def _(t):
        for s in range(2):
            for way in (1, -1):
                cond, copy = hid_moves(way, t, s)

                @pl.when(cond)
                def _():
                    copy.wait_send()

    @pl.loop(0, seg)
    def _(p):
        for s in range(2):
            hid_show(s, 2 * p + core).wait_send()

    @pl.loop(1, 2 * layers)
    def _(j):
        n = lax.rem(2 * layer + core + j, 2 * layers)
        home(n // 2, lax.rem(n, 2)).wait_send()


def run_experts(send, wgu, wd, nctx, nexp):
    xy = nexp // 2
    seg = nctx // 2
    layers = 2 * seg
    span = send.shape[1]
    width = 4 * span
    units = wgu.shape[0] // 2
    cols = wd.shape[1]
    dma = pltpu.SemaphoreType.DMA
    vm = pl.BlockSpec(memory_space=pltpu.VMEM)
    return pl.pallas_call(
        functools.partial(experts_kernel, nctx, nexp),
        out_shape=jax.ShapeDtypeStruct(send.shape, BF),
        in_specs=[vm] * 3,
        out_specs=vm,
        scratch_shapes=[
            pltpu.VMEM(send.shape, BF),
            pltpu.VMEM((layers, 2, 2, xy, width), BF),
            pltpu.VMEM((seg, 2, xy, width), BF),
            pltpu.VMEM((2, nctx, units, seg * 4 * xy), BF),
            pltpu.VMEM((layers, 2, 2 * xy, cols), BF),
            pltpu.VMEM((nctx // 4, 2, 4, 2 * xy, cols), BF),
            pltpu.VMEM(send.shape, BF),
            pltpu.VMEM(send.shape, BF),
            dma((xy,)),
            dma((xy,)),
            dma((2, layers, 2)),
            dma((layers, 2)),
            dma((2, layers, 2)),
            dma((seg, 2)),
            dma((layers, 2)),
            dma((layers, 2)),
            dma((2, layers, 2)),
            dma((2, nctx)),
            dma((2, nctx)),
            dma((2, nctx)),
            dma((2 * layers,)),
            dma((2 * layers,)),
            dma((xy,)),
            dma((xy,)),
        ],
        compiler_params=pltpu.CompilerParams(
            collective_id=1, has_side_effects=True, vmem_limit_bytes=48 << 20
        ),
    )(send, wgu, wd)


def join_kernel(experts, att_ref, back_ref, comb_ref, idr_ref, idc_ref, out_ref):
    tok, width = att_ref.shape
    count, span = back_ref.shape
    idr = idr_ref[0:1]
    idc = idc_ref[...]
    before = lax.broadcasted_iota(jnp.int32, (tok, tok), 1) < lax.broadcasted_iota(
        jnp.int32, (tok, tok), 0
    )
    earlier = jnp.sum(
        jnp.where(jnp.logical_and(before, idc == idr), 1, 0), axis=1, keepdims=True
    )
    slot = slots(idc, earlier, experts)
    r = lax.broadcasted_iota(jnp.int32, (tok, count), 1)
    match = wanted_slot(r, count // 16) == slot
    part = quarter_of(r)
    comb = comb_ref[...]
    for q in range(4):
        chooser = jnp.where(jnp.logical_and(match, part == q), 1.0, 0.0).astype(BF)
        picked = jnp.dot(chooser, back_ref[...], preferred_element_type=F32)
        at = slice(q * span, (q + 1) * span)
        out_ref[:, at] = (att_ref[:, at].astype(F32) + comb * picked).astype(BF)


def join(att, back, comb, idr, idc, experts):
    vm = pl.BlockSpec(memory_space=pltpu.VMEM)
    return pl.pallas_call(
        functools.partial(join_kernel, experts),
        out_shape=jax.ShapeDtypeStruct(att.shape, BF),
        in_specs=[vm] * 5,
        out_specs=vm,
        compiler_params=pltpu.CompilerParams(vmem_limit_bytes=24 << 20),
    )(att, back, comb, idr, idc)


def shards(query, keyval, doc_ids, route_ids, combine, w_gate_up, w_down):
    nctx = lax.axis_size("ctx")
    nexp = lax.axis_size("exp")
    tok = query.shape[1]
    units = w_gate_up.shape[2]
    kv, doc = spread(keyval[0], jnp.broadcast_to(doc_ids, (8, tok)), nctx)
    idr = jnp.broadcast_to(route_ids, (8, tok))
    idc = route_ids.reshape(tok, 1)
    att, send = attend(kv, doc, query[0], doc_ids.reshape(tok, 1), idr, idc, nexp)
    back = run_experts(send, w_gate_up[0].reshape(2 * units, -1), w_down[0], nctx, nexp)
    return join(att, back, combine.reshape(tok, 1), idr, idc, nexp)[None]


def solution(mesh):
    placed = (
        P("exp", "ctx", None),
        P("exp", None, "ctx", None),
        P("exp", "ctx"),
        P("exp", "ctx"),
        P("exp", "ctx"),
        P("exp", None, "ctx", None),
        P("exp", None, "ctx"),
    )
    return jax.shard_map(
        shards, mesh=mesh, in_specs=placed, out_specs=P("exp", "ctx", None), check_vma=False
    )
```

time: 691 us -> 227 us (0.33)
  the two profiles are of different devices: /device:TPU:33 before, /device:TPU:88 now
where the time goes in v1:
time: 227 us
  Pallas kernels  221 us (97%)
  local copies, waits for them, and re-layouts  5.2 us (2%)
    pallas_call x1, Pallas kernels, run_experts(): pl.pallas_call(functools.partial(experts_kernel, nctx, nexp), out_shape=j...  186 us
    pallas_call x1, Pallas kernels, spread(): pl.pallas_call(functools.partial(spread_kernel, nctx), out_shape=(jax.Sha...  24.8 us
    pallas_call x1, Pallas kernels, attend(): pl.pallas_call(functools.partial(attend_kernel, experts), out_shape=(jax....  8.48 us

profile of v1, /device:TPU:88, one launch (start us, length us, event | category | flops | bytes accessed | tf_op | source)
XLA Modules:
  0.0 226.6 jit_solution(877312892617492796)
XLA Ops:
  0.0 0.7 broadcast_in_dim.18.doc_ref
  0.7 0.0 copy-start.3
  0.7 0.9 copy-done.3
  1.6 24.8 %shard_map.73 = (bf16[2,2048,256]{2,1,0:T(8,128)(2,1)S(1)}, s32[16,8,128]{2,1,0:T(8,128)S(1)}) custom-call(bf16[2,128,256]{2,1,0:T(8,128)(2,1)S(1)} %bitcast.13, s32[8,128]{1,0:T(8,128)S(1)} %broadcast_in_dim.18.doc_ref), custom_call_target="tpu_custom_call" | custom-call | tf_op jit(solution)/shard_map/pallas_call | solution.py:139
  26.4 0.8 copy.9.idc_ref
  27.1 0.7 broadcast_in_dim.20.idr_ref
  27.8 0.8 copy.8.qdoc_ref
  28.6 0.0 copy-start
  28.6 0.0 copy-start.1
  28.6 1.3 copy-done.1
  29.9 0.0 copy-start.2
  29.9 8.5 %shard_map.74 = (bf16[128,4096]{1,0:T(8,128)(2,1)S(1)}, bf16[256,1024]{1,0:T(8,128)(2,1)S(1)}) custom-call(bf16[2,2048,256]{2,1,0:T(8,128)(2,1)S(1)} %get-tuple-element.9.kv_ref, s32[16,8,128]{2,1,0:T(8,128)S(1)} %get-tuple-element.10.doc_ref, bf16[128,4096]{1,0:T(8,128)(2,1)S(1)} %bitcast.11, s32[128,1]{1,0:T(8,128)S(1)} %copy.8.qdoc_ref, ...), custom_call_target="tpu_custom_call" | custom-call | tf_op jit(solution)/shard_map/pallas_call | solution.py:278
  38.4 0.0 copy-start.4
  38.4 0.0 copy-done
  38.4 0.0 copy-done.2
  38.4 186.4 %shard_map.75.back_ref = bf16[256,1024]{1,0:T(8,128)(2,1)S(1)} custom-call(bf16[256,1024]{1,0:T(8,128)(2,1)S(1)} %get-tuple-element.12.send_ref, bf16[192,4096]{1,0:T(8,128)(2,1)S(1)} %bitcast.10, bf16[1536,256]{1,0:T(8,128)(2,1)S(1)} %bitcast.12), custom_call_target="tpu_custom_call" | custom-call | tf_op jit(solution)/shard_map/pallas_call | solution.py:616
  224.8 0.0 copy-done.4
  224.8 0.1 copy.10.comb_ref
  225.0 1.7 shard_map.76
Async XLA Ops:
  0.7 0.9 copy-start.3
  28.6 9.9 %copy-start = (bf16[1,2,96,4096]{3,2,1,0:T(8,128)(2,1)S(1)}, bf16[1,2,96,4096]{3,2,1,0:T(8,128)(2,1)}, u32[]{:S(2)}) copy-start(bf16[1,2,96,4096]{3,2,1,0:T(8,128)(2,1)} %param.12) | copy-start | bytes 4718596
  28.6 1.3 copy-start.1
  29.9 8.5 %copy-start.2 = (bf16[1,1536,256]{2,1,0:T(8,128)(2,1)S(1)}, bf16[1,1536,256]{2,1,0:T(8,128)(2,1)}, u32[]{:S(2)}) copy-start(bf16[1,1536,256]{2,1,0:T(8,128)(2,1)} %param.13) | copy-start | bytes 2359300
  38.4 186.4 %copy-start.4 = (f32[1,128]{1,0:T(1,128)S(1)}, f32[1,128]{1,0:T(1,128)}, u32[]{:S(2)}) copy-start(f32[1,128]{1,0:T(1,128)} %param.11) | copy-start | bytes 1540

commit v2 on v1

--- a/solution.py
+++ b/solution.py
@@ -17,6 +17,7 @@
 BF = jnp.bfloat16
 F32 = jnp.float32
 MESH = pl.DeviceIdType.MESH
+HBM = pltpu.HBM
 NT = (((1,), (1,)), ((), ()))
 TN = (((0,), (0,)), ((), ()))
 
@@ -33,7 +34,8 @@
 
 
 def spread_kernel(
-    nctx, kv_ref, doc_ref, kv_out, doc_out, got, got_doc, sent, sent_doc, shown, shown_doc
+    nctx, kv_ref, doc_ref, w_ref, kv_out, doc_out, w_out,
+    got, got_doc, sent, sent_doc, shown, shown_doc, kept, w_sent, w_got,
 ):
     tok = kv_ref.shape[1]
     seg = nctx // 2
@@ -72,7 +74,7 @@
             out.append(
                 remote(src, kv_out.at[part, block(b)], sems.at[part], got.at[b, part], target)
             )
-        src = doc_ref if first else doc_out.at[b]
+        src = doc_ref.at[0:1] if first else doc_out.at[b]
         out.append(remote(src, doc_out.at[b], doc_sem, got_doc.at[b], target))
         return out
 
@@ -92,8 +94,26 @@
 
     for copy in across(ctx, True):
         copy.start()
-    kv_out[:, block(ctx), :] = kv_ref[...]
-    doc_out[ctx] = doc_ref[...]
+    idle = jnp.logical_or(pos == 0, pos == seg - 1)
+    near = jnp.logical_or(pos == 1, pos == seg - 2)
+    inwards = jnp.where(pos < seg // 2, ctx + 2, ctx - 2)
+    early = w_out.shape[0] // 16
+
+    def weights(i):
+        part = pl.ds(i * 16, 16)
+        return remote(w_ref.at[part], w_out.at[part], w_sent.at[i], w_got.at[i], (inwards, exp))
+
+    @pl.when(idle)
+    def _():
+        for i in range(early):
+            weights(i).start()
+
+    own = [
+        pltpu.make_async_copy(kv_ref, kv_out.at[:, block(ctx)], kept.at[0]),
+        pltpu.make_async_copy(doc_ref, doc_out.at[ctx], kept.at[1]),
+    ]
+    for copy in own:
+        copy.start()
 
     for t in range(1, reach + 1):
         for way in (1, -1):
@@ -113,6 +133,19 @@
                             on[n].start()
 
                     there[n].start()
+
+    for copy in own:
+        copy.wait()
+
+    @pl.when(idle)
+    def _():
+        for i in range(early):
+            weights(i).wait_send()
+
+    @pl.when(near)
+    def _():
+        for i in range(early):
+            weights(i).wait_recv()
 
     for t in range(0, reach + 1):
         for way in (1, -1):
@@ -134,16 +167,18 @@
                             copy.wait_send()
 
 
-def spread(kv, doc, nctx):
+def spread(kv, doc, wgu, nctx):
+    early = max(1, wgu.shape[0] // 16 * 5 // 12)
     _, tok, width = kv.shape
     return pl.pallas_call(
         functools.partial(spread_kernel, nctx),
         out_shape=(
             jax.ShapeDtypeStruct((2, nctx * tok, width), BF),
-            jax.ShapeDtypeStruct((nctx, 8, tok), jnp.int32),
+            jax.ShapeDtypeStruct((nctx, 1, tok), jnp.int32),
+            jax.ShapeDtypeStruct((16 * early, wgu.shape[1]), BF),
         ),
-        in_specs=[pl.BlockSpec(memory_space=pltpu.VMEM)] * 2,
-        out_specs=(pl.BlockSpec(memory_space=pltpu.VMEM),) * 2,
+        in_specs=[pl.BlockSpec(memory_space=HBM)] * 3,
+        out_specs=(pl.BlockSpec(memory_space=pltpu.VMEM),) * 3,
         scratch_shapes=[
             pltpu.SemaphoreType.DMA((nctx, 2)),
             pltpu.SemaphoreType.DMA((nctx,)),
@@ -151,11 +186,14 @@
             pltpu.SemaphoreType.DMA((2, 8)),
             pltpu.SemaphoreType.DMA((nctx, 2)),
             pltpu.SemaphoreType.DMA((nctx,)),
+            pltpu.SemaphoreType.DMA((2,)),
+            pltpu.SemaphoreType.DMA((early,)),
+            pltpu.SemaphoreType.DMA((early,)),
         ],
         compiler_params=pltpu.CompilerParams(
             collective_id=0, has_side_effects=True, vmem_limit_bytes=16 << 20
         ),
-    )(kv, doc)
+    )(kv, doc, wgu)
 
 
 def wanted_slot(r, columns):
@@ -167,16 +205,33 @@
     return lax.rem(r, 16) // 4
 
 
+def column(row):
+    n = row.shape[1]
+    return jnp.transpose(jnp.broadcast_to(row, (n, n)))[:, :1]
+
+
 def slots(ids, earlier, experts):
     kept = jnp.logical_and(ids < experts, earlier < CAP)
     return jnp.where(kept, ids * CAP + earlier, -1)
 
 
 def attend_kernel(
-    experts, kv_ref, doc_ref, q_ref, qdoc_ref, idr_ref, idc_ref, att_ref, send_ref, s_scr, m_scr, l_scr, a_scr
+    experts, kv_ref, doc_ref, q_hbm, id_hbm, att_ref, send_ref, q_ref, id_ref, s_scr, m_scr, l_scr, a_scr, q_got
 ):
     tok, width = q_ref.shape
     nctx = doc_ref.shape[0]
+    share = width // (kv_ref.shape[2] // HD)
+    loads = [
+        pltpu.make_async_copy(
+            q_hbm.at[:, g * share : (g + 1) * share],
+            q_ref.at[:, g * share : (g + 1) * share],
+            q_got.at[g],
+        )
+        for g in range(width // share)
+    ]
+    loads.append(pltpu.make_async_copy(id_hbm, id_ref, q_got.at[len(loads)]))
+    for load in loads:
+        load.start()
     groups = kv_ref.shape[2] // HD
     per = width // HD // groups
     step = 2 * tok
@@ -185,19 +240,21 @@
     pos = lax.axis_index("ctx") // 2
     scale = HD ** (-0.5) * LOG2E
 
-    where = lax.broadcasted_iota(jnp.int32, (nctx, 8, tok), 0) // 2
+    where = lax.broadcasted_iota(jnp.int32, (nctx, 1, tok), 0) // 2
     docs = jnp.where(where < pos - reach, -1, jnp.where(where > pos + reach, 1 << 20, doc_ref[...]))
-    qdoc = qdoc_ref[...]
+    qdoc = doc_ref[lax.axis_index("ctx")]
     low = jnp.min(qdoc)
     high = jnp.max(qdoc)
-    begin = jnp.sum((docs < low).astype(jnp.int32)) // 8
-    end = jnp.sum((docs <= high).astype(jnp.int32)) // 8
+    begin = jnp.sum((docs < low).astype(jnp.int32))
+    end = jnp.sum((docs <= high).astype(jnp.int32))
+    qdoc = column(qdoc)
     first = begin // step
     last = (end + step - 1) // step
 
     squares = jnp.zeros((tok, HD), F32)
     for g in range(groups):
         lanes = slice(g * HD, (g + 1) * HD)
+        loads[g].wait()
         m_scr[...] = jnp.full(m_scr.shape, LOWEST, F32)
         l_scr[...] = jnp.zeros(l_scr.shape, F32)
         a_scr[...] = jnp.zeros(a_scr.shape, F32)
@@ -244,9 +301,10 @@
             wide = mixed.astype(F32)
             squares = squares + wide * wide
 
+    loads[-1].wait()
     inverse = lax.rsqrt(jnp.sum(squares, axis=1, keepdims=True) / width + EPS)
-    idr = idr_ref[0:1]
-    idc = idc_ref[...]
+    idr = id_ref[...]
+    idc = column(idr)
     before = lax.broadcasted_iota(jnp.int32, (tok, tok), 0) < lax.broadcasted_iota(
         jnp.int32, (tok, tok), 1
     )
@@ -269,7 +327,7 @@
         send_ref[:, piece : piece + 256] = total.astype(BF)
 
 
-def attend(kv, doc, q, qdoc, idr, idc, experts):
+def attend(kv, doc, q, ids, experts):
     tok, width = q.shape
     nctx = doc.shape[0]
     per = width // HD // (kv.shape[2] // HD)
@@ -281,23 +339,26 @@
             jax.ShapeDtypeStruct((tok, width), BF),
             jax.ShapeDtypeStruct((count, width // 4), BF),
         ),
-        in_specs=[vm] * 6,
+        in_specs=[vm, vm] + [pl.BlockSpec(memory_space=HBM)] * 2,
         out_specs=(vm, vm),
         scratch_shapes=[
+            pltpu.VMEM((tok, width), BF),
+            pltpu.VMEM((1, tok), jnp.int32),
             pltpu.VMEM((nctx // 2, per * tok, 2 * tok), F32),
             pltpu.VMEM((per * tok, HD), F32),
             pltpu.VMEM((per * tok, HD), F32),
             pltpu.VMEM((per * tok, HD), F32),
+            pltpu.SemaphoreType.DMA((width // HD // per + 1,)),
         ],
         compiler_params=pltpu.CompilerParams(vmem_limit_bytes=48 << 20),
-    )(kv, doc, q, qdoc, idr, idc)
+    )(kv, doc, q, ids)
 
 
 def experts_kernel(
-    nctx, nexp, send_ref, wgu_ref, wd_ref, back_ref,
-    came, rows, transit, hid, made, ret, send2, back,
+    nctx, nexp, send_ref, wgu_ref, wd_ref, early_ref, back_ref,
+    came, rows, transit, hid0, hid1, made, ret, send2, back,
     a_sent, a_got, r_sent, r_got, t_sent, t_got, x_sent, x_got,
-    h_sent, h_got, y_sent, y_got, d_sent, d_got, b_sent, b_got,
+    h_sent, h_got, y_sent, y_got, d_sent, d_got, b_sent, b_got, wx, w_sent, w_got,
 ):
     seg = nctx // 2
     half = seg // 2
@@ -317,6 +378,18 @@
     layers = 2 * seg
     sibling = (ctx + 1 - 2 * core, exp)
 
+    idle = jnp.logical_or(pos == 0, pos == seg - 1)
+    near = jnp.logical_or(pos == 1, pos == seg - 2)
+    beside = jnp.where(pos < half, ctx + 2, ctx - 2)
+    outer = jnp.where(pos < half, ctx - 2, ctx + 2)
+    parts = 2 * units // 16
+    early = early_ref.shape[0] // 16
+    ahead = early + min(parts // 3, parts - early)
+
+    def weights(i, target):
+        part = pl.ds(pl.multiple_of(i * 16, 16), 16)
+        return remote(wgu_ref.at[part], wx.at[part], w_sent.at[i], w_got.at[i], (target, exp))
+
     def at_layer(z, c):
         z = lax.rem(z + 2 * layers, layers)
         return (2 * lax.rem(z, seg) + c, (z // seg) * xy + place)
@@ -365,6 +438,15 @@
         @pl.loop(1, xy)
         def _(j):
             swap(src, dst, sent, got, lax.rem(place + j, xy))[0].wait_send()
+
+    @pl.when(idle)
+    def _():
+        for i in range(early, ahead):
+            weights(i, beside).start()
+
+    @pl.when(near)
+    def _():
+        wx[: 16 * early] = early_ref[...]
 
     exchange(send_ref, came, a_sent, a_got)
     r = lax.broadcasted_iota(jnp.int32, (2 * xy, 16 * xy), 0)
@@ -405,7 +487,7 @@
                 remote(transit.at[p, h], rows.at[z, core, h], t_sent.at[d, t, h], r_got.at[z, h], target),
             ),
             (
-                jnp.logical_and(k < seg - 1, t <= k + 1 + half),
+                jnp.logical_and(k < seg - 2, t <= k + 1 + half),
                 remote(rows.at[z, core, h], rows.at[z, core, h], r_sent.at[d, t, h], r_got.at[z, h], target),
             ),
         ]
@@ -423,12 +505,18 @@
     for h in range(2):
         for way in (1, -1):
             chunk_start(way, 1, h)
-        show(layer, h, core).start()
-
-    steps = seg - 1 + half
-
-    @pl.loop(1, steps + 1)
-    def _(t):
+        pl.when(jnp.logical_not(idle))(show(layer, h, core).start)
+
+    steps = seg - 2 + half
+
+    def rows_step(t):
+        for j in range(2):
+            i = ahead + 2 * (t - 1) + j
+
+            @pl.when(jnp.logical_and(idle, i < parts))
+            def _():
+                weights(i, beside).start()
+
         for h in range(2):
             for way in (1, -1):
                 k = rank_of(way)
@@ -441,7 +529,9 @@
                         transit.at[p, h], transit.at[p, h], t_sent.at[0, 0, h], t_got.at[p, h], sibling
                     ).wait_recv()
 
-                @pl.when(t <= k + half)
+                needed = jnp.logical_and(k < seg - 1, t <= k + half)
+
+                @pl.when(needed)
                 def _():
                     remote(
                         rows.at[z, core, h], rows.at[z, core, h], r_sent.at[0, 0, h], r_got.at[z, h], sibling
@@ -449,64 +539,120 @@
 
                 chunk_start(way, t + 1, h)
 
-                @pl.when(t <= k + half)
+                @pl.when(jnp.logical_and(needed, jnp.logical_not(idle)))
                 def _():
                     show(z, h, core).start()
 
-    @pl.loop(0, layers)
-    def _(z):
-        for h in range(2):
-            show(z, h, 1 - core).wait_recv()
-
-    def hid_moves(way, t, s):
+    mine, other = zhi, 1 - zhi
+    quart = half // 2
+    sizes = (seg, half, half)
+
+    def layer_of(g, j):
+        if g == 0:
+            return mine * seg + j
+        if g == 1:
+            return other * seg + j + jnp.where(j >= quart, seg - half, 0)
+        return other * seg + quart + j
+
+    def ranges(g):
+        if g == 0:
+            return [(mine * seg, seg, 0)]
+        if g == 1:
+            return [(other * seg, quart, 0), (other * seg + seg - quart, quart, quart)]
+        return [(other * seg + quart, half, 0)]
+
+    def rows_shown(g):
+        @pl.when(jnp.logical_not(idle))
+        def _():
+            @pl.loop(0, sizes[g])
+            def _(j):
+                for h in range(2):
+                    show(layer_of(g, j), h, 1 - core).wait_recv()
+
+    def hid(g, b):
+        return hid0.at[b] if g == 0 else hid1.at[g - 1, b]
+
+    def hid_move(g, b, sent, target):
+        return remote(hid(g, b), hid(g, b), sent, h_got.at[g, b], target)
+
+    def hid_came(g, b):
+        hid_move(g, b, h_sent.at[0, 0, g], sibling).wait_recv()
+
+    def hid_moves(way, t, g):
         d = 0 if way == 1 else 1
         k = rank_of(way)
         b = 2 * (pos - way * (t - 1)) + core
-        target = (ctx + 2 * way, exp)
         return (
-            jnp.logical_and(k < seg - 1, t <= k + 1),
-            remote(hid.at[s, b], hid.at[s, b], h_sent.at[d, t, s], h_got.at[s, b], target),
+            jnp.logical_and(jnp.logical_and(k > 0, k < seg - 1), t <= k + 1),
+            hid_move(g, b, h_sent.at[d, t, g], (ctx + 2 * way, exp)),
         )
 
-    def hid_start(way, t, s):
-        cond, copy = hid_moves(way, t, s)
+    def hid_start(way, t, g):
+        cond, copy = hid_moves(way, t, g)
 
         @pl.when(cond)
         def _():
             copy.start()
 
-    def hid_show(s, b):
-        return remote(hid.at[s, b], hid.at[s, b], y_sent.at[s, b], y_got.at[s, b], sibling)
+    def hid_show(g, b):
+        return remote(hid(g, b), hid(g, b), y_sent.at[g, b], y_got.at[g, b], sibling)
 
     chunk = 4 * xy
-    some = seg * chunk
-    for s in range(2):
-        x = rows[s * seg : (s + 1) * seg].reshape(some, width)
-        both = lax.dot_general(wgu_ref[...], x, NT, preferred_element_type=F32)
+
+    def hid_out(way, g):
+        d = 0 if way == 1 else 1
+        return hid_move(g, outer, h_sent.at[d, 0, g], (outer, exp))
+
+    def units_of(w, g):
+        x = [rows[pl.ds(z, n)].reshape(n * chunk, width) for z, n, _ in ranges(g)]
+        x = x[0] if len(x) == 1 else jnp.concatenate(x, axis=0)
+        both = lax.dot_general(w[...], x, NT, preferred_element_type=F32)
         gate, upper = both[:units], both[units:]
-        hid[s, ctx] = (gate / (1.0 + jnp.exp(-gate)) * upper).astype(BF)
+        return (gate / (1.0 + jnp.exp(-gate)) * upper).astype(BF)
+
+    def gate_up(g):
+        rows_shown(g)
+
+        @pl.when(jnp.logical_not(idle))
+        def _():
+            hid(g, ctx)[...] = units_of(wgu_ref, g)
+            for way in (1, -1):
+                hid_start(way, 1, g)
+            hid_show(g, ctx).start()
+
+        @pl.when(near)
+        def _():
+            if g == 0:
+
+                @pl.loop(early, parts)
+                def _(i):
+                    weights(i, outer).wait_recv()
+
+            hid(g, outer)[...] = units_of(wx, g)
+            for way in (1, -1):
+
+                @pl.when(rank_of(way) == 1)
+                def _():
+                    hid_out(way, g).start()
+                    hid_start(way, 2, g)
+
+            hid_show(g, outer).start()
+
+    def hid_step(g, t):
+        @pl.when(jnp.logical_and(idle, t == 1))
+        def _():
+            hid_came(g, ctx)
+            hid_show(g, ctx).start()
+
         for way in (1, -1):
-            hid_start(way, 1, s)
-        hid_show(s, ctx).start()
-
-    @pl.loop(1, seg)
-    def _(t):
-        for s in range(2):
-            for way in (1, -1):
-                k = rank_of(way)
-                b = 2 * (pos - way * t) + core
-
-                @pl.when(t <= k)
-                def _():
-                    remote(
-                        hid.at[s, b], hid.at[s, b], h_sent.at[0, 0, s], h_got.at[s, b], sibling
-                    ).wait_recv()
-
-                hid_start(way, t + 1, s)
-
-                @pl.when(t <= k)
-                def _():
-                    hid_show(s, b).start()
+            k = rank_of(way)
+            b = 2 * (pos - way * t) + core
+
+            @pl.when(jnp.logical_and(t <= k, k + t > 2))
+            def _():
+                hid_came(g, b)
+                hid_start(way, t + 1, g)
+                hid_show(g, b).start()
 
     fold = nctx // 4
 
@@ -523,25 +669,69 @@
         slot = (lax.rem(n_ctx, fold), z // seg, n_ctx // fold)
         return remote(made.at[z, c], ret.at[slot], d_sent.at[2 * z + c], d_got.at[n], at_layer(z, c))
 
-    for s in range(2):
-
+    def down(g):
         @pl.loop(0, seg)
         def _(p):
-            hid_show(s, 2 * p + 1 - core).wait_recv()
-
-        hidden = hid[s].reshape(nctx * units, some)
+            hid_show(g, 2 * p + 1 - core).wait_recv()
+
+        some = sizes[g] * chunk
+        hidden = (hid0[...] if g == 0 else hid1[g - 1]).reshape(nctx * units, some)
         out = lax.dot_general(hidden, wd_ref[...], TN, preferred_element_type=F32)
-        made[s * seg : (s + 1) * seg] = out.astype(BF).reshape(seg, 2, 2 * xy, cols)
-
-        me = 2 * layer + core
-
-        @pl.loop(0, nctx)
+        out = out.astype(BF).reshape(sizes[g], 2, 2 * xy, cols)
+        for z, n, j in ranges(g):
+            made[pl.ds(z, n)] = out[j : j + n]
+        count = 2 * sizes[g]
+
+        @pl.loop(0, count)
         def _(j):
-            n = lax.rem(me + j, nctx) + s * nctx
-
-            @pl.when(n != me)
+            n = lax.rem(ctx + j, count)
+            z, c = layer_of(g, n // 2), lax.rem(n, 2)
+
+            @pl.when(jnp.logical_or(z != layer, c != core))
             def _():
-                home(n // 2, lax.rem(n, 2)).start()
+                home(z, c).start()
+
+    @pl.loop(1, seg - 1)
+    def _(t):
+        rows_step(t)
+
+    gate_up(0)
+
+    @pl.loop(1, quart + 1)
+    def _(u):
+        rows_step(seg - 2 + u)
+        hid_step(0, u)
+
+    gate_up(1)
+
+    @pl.loop(quart + 1, half + 1)
+    def _(u):
+        rows_step(seg - 2 + u)
+        hid_step(0, u)
+        hid_step(1, u - quart)
+
+    gate_up(2)
+
+    @pl.loop(half + 1, seg)
+    def _(u):
+        hid_step(0, u)
+        hid_step(1, u - quart)
+        hid_step(2, u - half)
+
+    down(0)
+
+    @pl.loop(seg, seg + quart)
+    def _(u):
+        hid_step(1, u - quart)
+        hid_step(2, u - half)
+
+    down(1)
+
+    @pl.loop(seg + quart, seg + half)
+    def _(u):
+        hid_step(2, u - half)
+
+    down(2)
 
     ret[lax.rem(ctx, fold), zhi, ctx // fold] = made[layer, core]
 
@@ -577,16 +767,28 @@
                     def _():
                         copy.wait_send()
 
-    @pl.loop(0, layers)
-    def _(z):
-        for h in range(2):
-            show(z, h, core).wait_send()
+    @pl.when(jnp.logical_not(idle))
+    def _():
+        @pl.loop(0, layers)
+        def _(z):
+            for h in range(2):
+                show(z, h, core).wait_send()
+
+    @pl.when(idle)
+    def _():
+        @pl.loop(early, parts)
+        def _(i):
+            weights(i, beside).wait_send()
+
+    for way in (1, -1):
+        for g in range(3):
+            pl.when(rank_of(way) == 1)(hid_out(way, g).wait_send)
 
     @pl.loop(1, seg + 1)
     def _(t):
-        for s in range(2):
+        for g in range(3):
             for way in (1, -1):
-                cond, copy = hid_moves(way, t, s)
+                cond, copy = hid_moves(way, t, g)
 
                 @pl.when(cond)
                 def _():
@@ -594,8 +796,8 @@
 
     @pl.loop(0, seg)
     def _(p):
-        for s in range(2):
-            hid_show(s, 2 * p + core).wait_send()
+        for g in range(3):
+            hid_show(g, 2 * p + core).wait_send()
 
     @pl.loop(1, 2 * layers)
     def _(j):
@@ -603,7 +805,7 @@
         home(n // 2, lax.rem(n, 2)).wait_send()
 
 
-def run_experts(send, wgu, wd, nctx, nexp):
+def run_experts(send, wgu, wd, wx, nctx, nexp):
     xy = nexp // 2
     seg = nctx // 2
     layers = 2 * seg
@@ -616,13 +818,14 @@
     return pl.pallas_call(
         functools.partial(experts_kernel, nctx, nexp),
         out_shape=jax.ShapeDtypeStruct(send.shape, BF),
-        in_specs=[vm] * 3,
+        in_specs=[vm] * 4,
         out_specs=vm,
         scratch_shapes=[
             pltpu.VMEM(send.shape, BF),
             pltpu.VMEM((layers, 2, 2, xy, width), BF),
             pltpu.VMEM((seg, 2, xy, width), BF),
-            pltpu.VMEM((2, nctx, units, seg * 4 * xy), BF),
+            pltpu.VMEM((nctx, units, seg * 4 * xy), BF),
+            pltpu.VMEM((2, nctx, units, seg * 2 * xy), BF),
             pltpu.VMEM((layers, 2, 2 * xy, cols), BF),
             pltpu.VMEM((nctx // 4, 2, 4, 2 * xy, cols), BF),
             pltpu.VMEM(send.shape, BF),
@@ -635,26 +838,37 @@
             dma((seg, 2)),
             dma((layers, 2)),
             dma((layers, 2)),
-            dma((2, layers, 2)),
-            dma((2, nctx)),
-            dma((2, nctx)),
-            dma((2, nctx)),
+            dma((2, layers, 3)),
+            dma((3, nctx)),
+            dma((3, nctx)),
+            dma((3, nctx)),
             dma((2 * layers,)),
             dma((2 * layers,)),
             dma((xy,)),
             dma((xy,)),
+            pltpu.VMEM(wgu.shape, BF),
+            dma((2 * units // 16,)),
+            dma((2 * units // 16,)),
         ],
         compiler_params=pltpu.CompilerParams(
             collective_id=1, has_side_effects=True, vmem_limit_bytes=48 << 20
         ),
-    )(send, wgu, wd)
-
-
-def join_kernel(experts, att_ref, back_ref, comb_ref, idr_ref, idc_ref, out_ref):
+    )(send, wgu, wd, wx)
+
+
+def join_kernel(experts, att_ref, back_ref, comb_hbm, id_hbm, out_ref, comb_ref, id_ref, got):
+    loads = [
+        pltpu.make_async_copy(comb_hbm, comb_ref, got.at[0]),
+        pltpu.make_async_copy(id_hbm, id_ref, got.at[1]),
+    ]
+    for load in loads:
+        load.start()
+    for load in loads:
+        load.wait()
     tok, width = att_ref.shape
     count, span = back_ref.shape
-    idr = idr_ref[0:1]
-    idc = idc_ref[...]
+    idr = id_ref[...]
+    idc = column(idr)
     before = lax.broadcasted_iota(jnp.int32, (tok, tok), 1) < lax.broadcasted_iota(
         jnp.int32, (tok, tok), 0
     )
@@ -665,7 +879,7 @@
     r = lax.broadcasted_iota(jnp.int32, (tok, count), 1)
     match = wanted_slot(r, count // 16) == slot
     part = quarter_of(r)
-    comb = comb_ref[...]
+    comb = column(comb_ref[...])
     for q in range(4):
         chooser = jnp.where(jnp.logical_and(match, part == q), 1.0, 0.0).astype(BF)
         picked = jnp.dot(chooser, back_ref[...], preferred_element_type=F32)
@@ -673,28 +887,31 @@
         out_ref[:, at] = (att_ref[:, at].astype(F32) + comb * picked).astype(BF)
 
 
-def join(att, back, comb, idr, idc, experts):
+def join(att, back, comb, ids, experts):
     vm = pl.BlockSpec(memory_space=pltpu.VMEM)
     return pl.pallas_call(
         functools.partial(join_kernel, experts),
         out_shape=jax.ShapeDtypeStruct(att.shape, BF),
-        in_specs=[vm] * 5,
+        in_specs=[vm, vm] + [pl.BlockSpec(memory_space=HBM)] * 2,
         out_specs=vm,
+        scratch_shapes=[
+            pltpu.VMEM(comb.shape, F32),
+            pltpu.VMEM(ids.shape, jnp.int32),
+            pltpu.SemaphoreType.DMA((2,)),
+        ],
         compiler_params=pltpu.CompilerParams(vmem_limit_bytes=24 << 20),
-    )(att, back, comb, idr, idc)
+    )(att, back, comb, ids)
 
 
 def shards(query, keyval, doc_ids, route_ids, combine, w_gate_up, w_down):
     nctx = lax.axis_size("ctx")
     nexp = lax.axis_size("exp")
-    tok = query.shape[1]
     units = w_gate_up.shape[2]
-    kv, doc = spread(keyval[0], jnp.broadcast_to(doc_ids, (8, tok)), nctx)
-    idr = jnp.broadcast_to(route_ids, (8, tok))
-    idc = route_ids.reshape(tok, 1)
-    att, send = attend(kv, doc, query[0], doc_ids.reshape(tok, 1), idr, idc, nexp)
-    back = run_experts(send, w_gate_up[0].reshape(2 * units, -1), w_down[0], nctx, nexp)
-    return join(att, back, combine.reshape(tok, 1), idr, idc, nexp)[None]
+    wgu = w_gate_up[0].reshape(2 * units, -1)
+    kv, doc, wx = spread(keyval[0], doc_ids, wgu, nctx)
+    att, send = attend(kv, doc, query[0], route_ids, nexp)
+    back = run_experts(send, wgu, w_down[0], wx, nctx, nexp)
+    return join(att, back, combine, route_ids, nexp)[None]
 
 
 def solution(mesh):

time: 227 us -> 212 us (0.934)
  the two profiles are of different devices: /device:TPU:88 before, /device:TPU:64 now
where the time goes in v2:
time: 212 us
  Pallas kernels  207 us (98%)
  local copies, waits for them, and re-layouts  4.85 us (2%)
    pallas_call x1, Pallas kernels, run_experts(): pl.pallas_call(functools.partial(experts_kernel, nctx, nexp), out_shape=j...  165 us
    pallas_call x1, Pallas kernels, spread(): pl.pallas_call(functools.partial(spread_kernel, nctx), out_shape=(jax.Sha...  25 us
    pallas_call x1, Pallas kernels, attend(): pl.pallas_call(functools.partial(attend_kernel, experts), out_shape=(jax....  14.6 us
    unnamed x16, local copies, waits for them, and re-layouts  4.85 us

profile of v2, /device:TPU:64, one launch (start us, length us, event | category | flops | bytes accessed | tf_op | source)
XLA Modules:
  0.0 211.8 jit_solution(16976278157497545730)
XLA Ops:
  0.0 0.0 copy-start
  0.0 1.4 copy-done
  1.4 0.0 copy-start.4
  1.4 0.9 copy-done.4
  2.3 0.0 copy-start.6
  2.3 0.7 copy-done.6
  3.0 0.0 copy-start.1
  3.0 25.0 %shard_map.73 = (bf16[2,2048,256]{2,1,0:T(8,128)(2,1)S(1)}, s32[16,1,128]{2,1,0:T(1,128)S(1)}, bf16[80,4096]{1,0:T(8,128)(2,1)S(1)}) custom-call(bf16[2,128,256]{2,1,0:T(8,128)(2,1)S(1)} %bitcast.9, s32[1,128]{1,0:T(1,128)S(1)} %copy-done.6, bf16[192,4096]{1,0:T(8,128)(2,1)S(1)} %bitcast.5), custom_call_target="tpu_custom_call" | custom-call | tf_op jit(solution)/shard_map/pallas_call | solution.py:173
  28.0 0.0 copy-start.2
  28.0 1.2 copy-done.2
  29.2 0.0 copy-start.5
  29.2 0.7 copy-done.5
  29.8 0.0 copy-start.3
  29.8 14.6 %shard_map.74 = (bf16[128,4096]{1,0:T(8,128)(2,1)S(1)}, bf16[256,1024]{1,0:T(8,128)(2,1)S(1)}) custom-call(bf16[2,2048,256]{2,1,0:T(8,128)(2,1)S(1)} %get-tuple-element.10.kv_ref, s32[16,1,128]{2,1,0:T(1,128)S(1)} %get-tuple-element.11.doc_ref, bf16[128,4096]{1,0:T(8,128)(2,1)S(1)} %bitcast.7, s32[1,128]{1,0:T(1,128)S(1)} %copy-done.5), custom_call_target="tpu_custom_call" | custom-call | tf_op jit(solution)/shard_map/pallas_call | solution.py:336
  44.5 0.0 copy-start.7
  44.5 0.0 copy-done.1
  44.5 0.0 copy-done.3
  44.5 165.3 %shard_map.75.back_ref = bf16[256,1024]{1,0:T(8,128)(2,1)S(1)} custom-call(bf16[256,1024]{1,0:T(8,128)(2,1)S(1)} %get-tuple-element.13.send_ref, bf16[192,4096]{1,0:T(8,128)(2,1)S(1)} %bitcast.6, bf16[1536,256]{1,0:T(8,128)(2,1)S(1)} %bitcast.8, bf16[80,4096]{1,0:T(8,128)(2,1)S(1)} %get-tuple-element.14.early_ref), custom_call_target="tpu_custom_call" | custom-call | tf_op jit(solution)/shard_map/pallas_call | solution.py:818
  209.8 0.0 copy-done.7
  209.8 1.8 shard_map.76
Async XLA Ops:
  0.0 1.4 copy-start
  1.4 0.9 copy-start.4
  2.3 0.7 copy-start.6
  3.0 41.5 %copy-start.1 = (bf16[1,2,96,4096]{3,2,1,0:T(8,128)(2,1)S(1)}, bf16[1,2,96,4096]{3,2,1,0:T(8,128)(2,1)}, u32[]{:S(2)}) copy-start(bf16[1,2,96,4096]{3,2,1,0:T(8,128)(2,1)} %param.12) | copy-start | bytes 4718596
  28.0 1.2 copy-start.2
  29.2 0.7 copy-start.5
  29.8 14.7 %copy-start.3 = (bf16[1,1536,256]{2,1,0:T(8,128)(2,1)S(1)}, bf16[1,1536,256]{2,1,0:T(8,128)(2,1)}, u32[]{:S(2)}) copy-start(bf16[1,1536,256]{2,1,0:T(8,128)(2,1)} %param.13) | copy-start | bytes 2359300
  44.5 165.4 %copy-start.7 = (f32[1,128]{1,0:T(1,128)S(1)}, f32[1,128]{1,0:T(1,128)}, u32[]{:S(2)}) copy-start(f32[1,128]{1,0:T(1,128)} %comb_hbm.1) | copy-start | bytes 1540

commit v3 on v2

--- a/solution.py
+++ b/solution.py
@@ -115,39 +115,7 @@
     for copy in own:
         copy.start()
 
-    for t in range(1, reach + 1):
-        for way in (1, -1):
-            source = pos - way * t
-            b = 2 * source + core
-
-            @pl.when(has(source))
-            def _():
-                there = across(b, False)
-                on = along(way, t, b) if t < reach else None
-                for n in range(3):
-                    there[n].wait_recv()
-                    if on is not None:
-
-                        @pl.when(has(pos + way))
-                        def _():
-                            on[n].start()
-
-                    there[n].start()
-
-    for copy in own:
-        copy.wait()
-
-    @pl.when(idle)
-    def _():
-        for i in range(early):
-            weights(i).wait_send()
-
-    @pl.when(near)
-    def _():
-        for i in range(early):
-            weights(i).wait_recv()
-
-    for t in range(0, reach + 1):
+    def finish(t):
         for way in (1, -1):
             source = pos - way * t
             b = 2 * source + core
@@ -165,6 +133,44 @@
                     def _():
                         for copy in along(way, t, b):
                             copy.wait_send()
+
+    for t in range(1, reach + 1):
+        for way in (1, -1):
+            source = pos - way * t
+            b = 2 * source + core
+
+            @pl.when(has(source))
+            def _():
+                there = across(b, False)
+                on = along(way, t, b) if t < reach else None
+                for n in range(3):
+                    there[n].wait_recv()
+                    if on is not None:
+
+                        @pl.when(has(pos + way))
+                        def _():
+                            on[n].start()
+
+                    there[n].start()
+
+        if t >= 2:
+            finish(t - 2)
+
+    for copy in own:
+        copy.wait()
+
+    @pl.when(idle)
+    def _():
+        for i in range(early):
+            weights(i).wait_send()
+
+    @pl.when(near)
+    def _():
+        for i in range(early):
+            weights(i).wait_recv()
+
+    for t in range(max(0, reach - 1), reach + 1):
+        finish(t)
 
 
 def spread(kv, doc, wgu, nctx):
@@ -359,6 +365,7 @@
     came, rows, transit, hid0, hid1, made, ret, send2, back,
     a_sent, a_got, r_sent, r_got, t_sent, t_got, x_sent, x_got,
     h_sent, h_got, y_sent, y_got, d_sent, d_got, b_sent, b_got, wx, w_sent, w_got,
+    wdx, wd_sent, wd_got, made_x, dx_sent,
 ):
     seg = nctx // 2
     half = seg // 2
@@ -390,6 +397,11 @@
         part = pl.ds(pl.multiple_of(i * 16, 16), 16)
         return remote(wgu_ref.at[part], wx.at[part], w_sent.at[i], w_got.at[i], (target, exp))
 
+    def weights_down(i, target):
+        n = 2 * units
+        part = pl.ds(pl.multiple_of(i * n, n), n)
+        return remote(wd_ref.at[part], wdx.at[part], wd_sent.at[i], wd_got.at[i], (target, exp))
+
     def at_layer(z, c):
         z = lax.rem(z + 2 * layers, layers)
         return (2 * lax.rem(z, seg) + c, (z // seg) * xy + place)
@@ -430,6 +442,7 @@
 
         dst[block16(place)] = src[block16(place)]
 
+    def exchange_wait(src, dst, sent, got):
         @pl.loop(1, xy)
         def _(j):
             swap(src, dst, sent, got, lax.rem(place + xy - j, xy))[1].wait_recv()
@@ -449,6 +462,7 @@
         wx[: 16 * early] = early_ref[...]
 
     exchange(send_ref, came, a_sent, a_got)
+    exchange_wait(send_ref, came, a_sent, a_got)
     r = lax.broadcasted_iota(jnp.int32, (2 * xy, 16 * xy), 0)
     c = lax.broadcasted_iota(jnp.int32, (2 * xy, 16 * xy), 1)
     for side in range(2):
@@ -517,6 +531,12 @@
             def _():
                 weights(i, beside).start()
 
+            n = 2 * (t - 1 - half) + j
+
+            @pl.when(jnp.logical_and(idle, jnp.logical_and(n >= 0, n < seg)))
+            def _():
+                weights_down(n, beside).start()
+
         for h in range(2):
             for way in (1, -1):
                 k = rank_of(way)
@@ -583,7 +603,7 @@
         k = rank_of(way)
         b = 2 * (pos - way * (t - 1)) + core
         return (
-            jnp.logical_and(jnp.logical_and(k > 0, k < seg - 1), t <= k + 1),
+            jnp.logical_and(jnp.logical_and(k > 0, k < seg - 2), t <= k + 1),
             hid_move(g, b, h_sent.at[d, t, g], (ctx + 2 * way, exp)),
         )
 
@@ -598,10 +618,6 @@
         return remote(hid(g, b), hid(g, b), y_sent.at[g, b], y_got.at[g, b], sibling)
 
     chunk = 4 * xy
-
-    def hid_out(way, g):
-        d = 0 if way == 1 else 1
-        return hid_move(g, outer, h_sent.at[d, 0, g], (outer, exp))
 
     def units_of(w, g):
         x = [rows[pl.ds(z, n)].reshape(n * chunk, width) for z, n, _ in ranges(g)]
@@ -633,22 +649,16 @@
 
                 @pl.when(rank_of(way) == 1)
                 def _():
-                    hid_out(way, g).start()
                     hid_start(way, 2, g)
 
             hid_show(g, outer).start()
 
     def hid_step(g, t):
-        @pl.when(jnp.logical_and(idle, t == 1))
-        def _():
-            hid_came(g, ctx)
-            hid_show(g, ctx).start()
-
         for way in (1, -1):
             k = rank_of(way)
             b = 2 * (pos - way * t) + core
 
-            @pl.when(jnp.logical_and(t <= k, k + t > 2))
+            @pl.when(jnp.logical_and(k < seg - 1, jnp.logical_and(t <= k, k + t > 2)))
             def _():
                 hid_came(g, b)
                 hid_start(way, t + 1, g)
@@ -656,30 +666,33 @@
 
     fold = nctx // 4
 
-    def home(z, c):
-        slot = (lax.rem(ctx, fold), zhi, ctx // fold)
-        n = zhi * nctx + ctx
+    def slot_of(z, c):
+        n = 2 * lax.rem(z, seg) + c
+        return lax.rem(n, fold), z // seg, n // fold
+
+    def home(source, sent, owner, z, c):
+        n = zhi * nctx + owner
+        slot = slot_of(zhi * seg + owner // 2, core)
+        return remote(source.at[z, c], ret.at[slot], sent.at[2 * z + c], d_got.at[n], at_layer(z, c))
+
+    def home_own(z, c):
+        return home(made, d_sent, ctx, z, c)
+
+    def home_outer(z, c):
+        return home(made_x, dx_sent, outer, z, c)
+
+    def home_from(z, c):
+        n = (z // seg) * nctx + 2 * lax.rem(z, seg) + c
         return remote(
-            made.at[z, c], ret.at[slot], d_sent.at[2 * z + c], d_got.at[n], at_layer(z, c)
+            made.at[z, c], ret.at[slot_of(z, c)], d_sent.at[2 * z + c], d_got.at[n], at_layer(z, c)
         )
 
-    def home_from(z, c):
-        n_ctx = 2 * lax.rem(z, seg) + c
-        n = (z // seg) * nctx + n_ctx
-        slot = (lax.rem(n_ctx, fold), z // seg, n_ctx // fold)
-        return remote(made.at[z, c], ret.at[slot], d_sent.at[2 * z + c], d_got.at[n], at_layer(z, c))
-
-    def down(g):
-        @pl.loop(0, seg)
-        def _(p):
-            hid_show(g, 2 * p + 1 - core).wait_recv()
-
-        some = sizes[g] * chunk
-        hidden = (hid0[...] if g == 0 else hid1[g - 1]).reshape(nctx * units, some)
-        out = lax.dot_general(hidden, wd_ref[...], TN, preferred_element_type=F32)
+    def send_home(g, w, into, move):
+        hidden = (hid0[...] if g == 0 else hid1[g - 1]).reshape(nctx * units, sizes[g] * chunk)
+        out = lax.dot_general(hidden, w[...], TN, preferred_element_type=F32)
         out = out.astype(BF).reshape(sizes[g], 2, 2 * xy, cols)
         for z, n, j in ranges(g):
-            made[pl.ds(z, n)] = out[j : j + n]
+            into[pl.ds(z, n)] = out[j : j + n]
         count = 2 * sizes[g]
 
         @pl.loop(0, count)
@@ -689,7 +702,26 @@
 
             @pl.when(jnp.logical_or(z != layer, c != core))
             def _():
-                home(z, c).start()
+                move(z, c).start()
+
+    def down(g):
+        @pl.when(jnp.logical_not(idle))
+        def _():
+            @pl.loop(0, seg)
+            def _(p):
+                hid_show(g, 2 * p + 1 - core).wait_recv()
+
+            send_home(g, wd_ref, made, home_own)
+
+        @pl.when(near)
+        def _():
+            if g == 0:
+
+                @pl.loop(0, seg)
+                def _(i):
+                    weights_down(i, outer).wait_recv()
+
+            send_home(g, wdx, made_x, home_outer)
 
     @pl.loop(1, seg - 1)
     def _(t):
@@ -712,7 +744,7 @@
 
     gate_up(2)
 
-    @pl.loop(half + 1, seg)
+    @pl.loop(half + 1, seg - 1)
     def _(u):
         hid_step(0, u)
         hid_step(1, u - quart)
@@ -720,25 +752,85 @@
 
     down(0)
 
-    @pl.loop(seg, seg + quart)
+    @pl.loop(seg - 1, seg - 1 + quart)
     def _(u):
         hid_step(1, u - quart)
         hid_step(2, u - half)
 
     down(1)
 
-    @pl.loop(seg + quart, seg + half)
+    @pl.loop(seg - 1 + quart, seg - 1 + half)
     def _(u):
         hid_step(2, u - half)
 
     down(2)
 
-    ret[lax.rem(ctx, fold), zhi, ctx // fold] = made[layer, core]
-
-    @pl.loop(1, 2 * layers)
-    def _(j):
-        n = lax.rem(2 * layer + core + j, 2 * layers)
-        home_from(n // 2, lax.rem(n, 2)).wait_recv()
+    exchange_end(send_ref, came, a_sent, a_got)
+
+    @pl.loop(1, steps + 2)
+    def _(t):
+        for h in range(2):
+            for way in (1, -1):
+                for cond, copy in chunk_moves(way, t, h):
+
+                    @pl.when(cond)
+                    def _():
+                        copy.wait_send()
+
+    @pl.when(jnp.logical_not(idle))
+    def _():
+        @pl.loop(0, layers)
+        def _(z):
+            for h in range(2):
+                show(z, h, core).wait_send()
+
+    @pl.when(idle)
+    def _():
+        @pl.loop(early, parts)
+        def _(i):
+            weights(i, beside).wait_send()
+
+        @pl.loop(0, seg)
+        def _(i):
+            weights_down(i, beside).wait_send()
+
+    @pl.loop(1, seg + 1)
+    def _(t):
+        for g in range(3):
+            for way in (1, -1):
+                cond, copy = hid_moves(way, t, g)
+
+                @pl.when(cond)
+                def _():
+                    copy.wait_send()
+
+    @pl.when(jnp.logical_not(idle))
+    def _():
+        @pl.loop(0, seg)
+        def _(p):
+            for g in range(3):
+                hid_show(g, 2 * p + core).wait_send()
+
+    @pl.when(jnp.logical_not(idle))
+    def _():
+        ret[slot_of(layer, core)] = made[layer, core]
+
+    @pl.when(near)
+    def _():
+        ret[slot_of(zhi * seg + outer // 2, core)] = made_x[layer, core]
+
+    @pl.loop(0, 2 * layers)
+    def _(n):
+        z, c = n // 2, lax.rem(n, 2)
+        p = z - zhi * seg
+        local = jnp.logical_or(
+            jnp.logical_and(jnp.logical_not(idle), p == pos),
+            jnp.logical_and(near, p == outer // 2),
+        )
+
+        @pl.when(jnp.logical_not(jnp.logical_and(local, c == core)))
+        def _():
+            home_from(z, c).wait_recv()
 
     r = lax.broadcasted_iota(jnp.int32, (16 * xy, 16 * xy), 0)
     c = lax.broadcasted_iota(jnp.int32, (16 * xy, 16 * xy), 1)
@@ -752,57 +844,24 @@
             place_back, got, preferred_element_type=F32
         ).astype(BF)
     exchange(send2, back, b_sent, b_got)
+
+    @pl.when(jnp.logical_not(idle))
+    def _():
+        @pl.loop(1, 2 * layers)
+        def _(j):
+            n = lax.rem(2 * layer + core + j, 2 * layers)
+            home_own(n // 2, lax.rem(n, 2)).wait_send()
+
+    @pl.when(near)
+    def _():
+        @pl.loop(1, 2 * layers)
+        def _(j):
+            n = lax.rem(2 * layer + core + j, 2 * layers)
+            home_outer(n // 2, lax.rem(n, 2)).wait_send()
+
+    exchange_wait(send2, back, b_sent, b_got)
     back_ref[...] = back[...]
-
-    exchange_end(send_ref, came, a_sent, a_got)
     exchange_end(send2, back, b_sent, b_got)
-
-    @pl.loop(1, steps + 2)
-    def _(t):
-        for h in range(2):
-            for way in (1, -1):
-                for cond, copy in chunk_moves(way, t, h):
-
-                    @pl.when(cond)
-                    def _():
-                        copy.wait_send()
-
-    @pl.when(jnp.logical_not(idle))
-    def _():
-        @pl.loop(0, layers)
-        def _(z):
-            for h in range(2):
-                show(z, h, core).wait_send()
-
-    @pl.when(idle)
-    def _():
-        @pl.loop(early, parts)
-        def _(i):
-            weights(i, beside).wait_send()
-
-    for way in (1, -1):
-        for g in range(3):
-            pl.when(rank_of(way) == 1)(hid_out(way, g).wait_send)
-
-    @pl.loop(1, seg + 1)
-    def _(t):
-        for g in range(3):
-            for way in (1, -1):
-                cond, copy = hid_moves(way, t, g)
-
-                @pl.when(cond)
-                def _():
-                    copy.wait_send()
-
-    @pl.loop(0, seg)
-    def _(p):
-        for g in range(3):
-            hid_show(g, 2 * p + core).wait_send()
-
-    @pl.loop(1, 2 * layers)
-    def _(j):
-        n = lax.rem(2 * layer + core + j, 2 * layers)
-        home(n // 2, lax.rem(n, 2)).wait_send()
 
 
 def run_experts(send, wgu, wd, wx, nctx, nexp):
@@ -849,6 +908,11 @@
             pltpu.VMEM(wgu.shape, BF),
             dma((2 * units // 16,)),
             dma((2 * units // 16,)),
+            pltpu.VMEM(wd.shape, BF),
+            dma((nctx // 2,)),
+            dma((nctx // 2,)),
+            pltpu.VMEM((layers, 2, 2 * xy, cols), BF),
+            dma((2 * layers,)),
         ],
         compiler_params=pltpu.CompilerParams(
             collective_id=1, has_side_effects=True, vmem_limit_bytes=48 << 20

time: 212 us -> 210 us (level)
  Pallas kernels: 207 us -> 204 us
where the time goes in v3:
time: 210 us; the launch traced here: 209 us
  Pallas kernels  204 us (97%)
  local copies, waits for them, and re-layouts  4.85 us (2%)
    pallas_call x1, Pallas kernels, run_experts(): pl.pallas_call(functools.partial(experts_kernel, nctx, nexp), out_shape=j...  165 us
    pallas_call x1, Pallas kernels, spread(): pl.pallas_call(functools.partial(spread_kernel, nctx), out_shape=(jax.Sha...  25 us
    pallas_call x1, Pallas kernels, attend(): pl.pallas_call(functools.partial(attend_kernel, experts), out_shape=(jax....  12.7 us
    unnamed x16, local copies, waits for them, and re-layouts  4.85 us

profile of v3, /device:TPU:64, one launch (start us, length us, event | category | flops | bytes accessed | tf_op | source)
XLA Modules:
  0.0 209.4 jit_solution(1378504526289084207)
XLA Ops:
  0.0 0.0 copy-start
  0.0 1.4 copy-done
  1.4 0.0 copy-start.4
  1.4 0.9 copy-done.4
  2.3 0.0 copy-start.6
  2.3 0.7 copy-done.6
  3.0 0.0 copy-start.1
  3.0 25.0 %shard_map.73 = (bf16[2,2048,256]{2,1,0:T(8,128)(2,1)S(1)}, s32[16,1,128]{2,1,0:T(1,128)S(1)}, bf16[80,4096]{1,0:T(8,128)(2,1)S(1)}) custom-call(bf16[2,128,256]{2,1,0:T(8,128)(2,1)S(1)} %bitcast.9, s32[1,128]{1,0:T(1,128)S(1)} %copy-done.6, bf16[192,4096]{1,0:T(8,128)(2,1)S(1)} %bitcast.5), custom_call_target="tpu_custom_call" | custom-call | tf_op jit(solution)/shard_map/pallas_call | solution.py:179
  28.0 0.0 copy-start.2
  28.0 1.2 copy-done.2
  29.2 0.0 copy-start.5
  29.2 0.7 copy-done.5
  29.8 0.0 copy-start.3
  29.8 12.7 %shard_map.74 = (bf16[128,4096]{1,0:T(8,128)(2,1)S(1)}, bf16[256,1024]{1,0:T(8,128)(2,1)S(1)}) custom-call(bf16[2,2048,256]{2,1,0:T(8,128)(2,1)S(1)} %get-tuple-element.10.kv_ref, s32[16,1,128]{2,1,0:T(1,128)S(1)} %get-tuple-element.11.doc_ref, bf16[128,4096]{1,0:T(8,128)(2,1)S(1)} %bitcast.7, s32[1,128]{1,0:T(1,128)S(1)} %copy-done.5), custom_call_target="tpu_custom_call" | custom-call | tf_op jit(solution)/shard_map/pallas_call | solution.py:342
  42.6 0.0 copy-start.7
  42.6 0.0 copy-done.1
  42.6 0.0 copy-done.3
  42.6 164.9 %shard_map.75.back_ref = bf16[256,1024]{1,0:T(8,128)(2,1)S(1)} custom-call(bf16[256,1024]{1,0:T(8,128)(2,1)S(1)} %get-tuple-element.13.send_ref, bf16[192,4096]{1,0:T(8,128)(2,1)S(1)} %bitcast.6, bf16[1536,256]{1,0:T(8,128)(2,1)S(1)} %bitcast.8, bf16[80,4096]{1,0:T(8,128)(2,1)S(1)} %get-tuple-element.14.early_ref), custom_call_target="tpu_custom_call" | custom-call | tf_op jit(solution)/shard_map/pallas_call | solution.py:877
  207.5 0.0 copy-done.7
  207.5 1.8 shard_map.76
Async XLA Ops:
  0.0 1.4 copy-start
  1.4 0.9 copy-start.4
  2.3 0.7 copy-start.6
  3.0 39.6 %copy-start.1 = (bf16[1,2,96,4096]{3,2,1,0:T(8,128)(2,1)S(1)}, bf16[1,2,96,4096]{3,2,1,0:T(8,128)(2,1)}, u32[]{:S(2)}) copy-start(bf16[1,2,96,4096]{3,2,1,0:T(8,128)(2,1)} %param.12) | copy-start | bytes 4718596
  28.0 1.2 copy-start.2
  29.2 0.7 copy-start.5
  29.8 12.8 %copy-start.3 = (bf16[1,1536,256]{2,1,0:T(8,128)(2,1)S(1)}, bf16[1,1536,256]{2,1,0:T(8,128)(2,1)}, u32[]{:S(2)}) copy-start(bf16[1,1536,256]{2,1,0:T(8,128)(2,1)} %param.13) | copy-start | bytes 2359300
  42.6 164.9 %copy-start.7 = (f32[1,128]{1,0:T(1,128)S(1)}, f32[1,128]{1,0:T(1,128)}, u32[]{:S(2)}) copy-start(f32[1,128]{1,0:T(1,128)} %comb_hbm.1) | copy-start | bytes 1540

commit v4 on v3

--- a/solution.py
+++ b/solution.py
@@ -249,13 +249,15 @@
     where = lax.broadcasted_iota(jnp.int32, (nctx, 1, tok), 0) // 2
     docs = jnp.where(where < pos - reach, -1, jnp.where(where > pos + reach, 1 << 20, doc_ref[...]))
     qdoc = doc_ref[lax.axis_index("ctx")]
-    low = jnp.min(qdoc)
-    high = jnp.max(qdoc)
-    begin = jnp.sum((docs < low).astype(jnp.int32))
-    end = jnp.sum((docs <= high).astype(jnp.int32))
+    part = tok // 2
+    spans = []
+    for p in range(2):
+        low = jnp.min(qdoc[:, p * part : (p + 1) * part])
+        high = jnp.max(qdoc[:, p * part : (p + 1) * part])
+        begin = jnp.sum((docs < low).astype(jnp.int32))
+        end = jnp.sum((docs <= high).astype(jnp.int32))
+        spans.append((begin // step, (end + step - 1) // step))
     qdoc = column(qdoc)
-    first = begin // step
-    last = (end + step - 1) // step
 
     squares = jnp.zeros((tok, HD), F32)
     for g in range(groups):
@@ -265,19 +267,21 @@
         l_scr[...] = jnp.zeros(l_scr.shape, F32)
         a_scr[...] = jnp.zeros(a_scr.shape, F32)
 
-        @pl.loop(first, last)
-        def _(kb):
-            keys = kv_ref[0, pl.ds(pl.multiple_of(kb * step, step), step), lanes]
-            kdoc = jnp.concatenate([doc_ref[2 * kb, 0:1], doc_ref[2 * kb + 1, 0:1]], axis=1)
-            bias = jnp.where(kdoc == qdoc, 0.0, LOWEST).astype(F32)
-            for h in range(per):
-                at = slice((g * per + h) * HD, (g * per + h + 1) * HD)
-                rows = slice(h * tok, (h + 1) * tok)
-                s = lax.dot_general(q_ref[:, at], keys, NT, preferred_element_type=F32) + bias
-                s_scr[kb, rows] = s
-                m_scr[rows] = jnp.maximum(
-                    m_scr[rows], jnp.maximum(s[:, :HD], s[:, HD:])
-                )
+        for p in range(2):
+
+            @pl.loop(*spans[p])
+            def _(kb):
+                keys = kv_ref[0, pl.ds(pl.multiple_of(kb * step, step), step), lanes]
+                kdoc = jnp.concatenate([doc_ref[2 * kb, 0:1], doc_ref[2 * kb + 1, 0:1]], axis=1)
+                bias = jnp.where(kdoc == qdoc[p * part : (p + 1) * part], 0.0, LOWEST).astype(F32)
+                for h in range(per):
+                    at = slice((g * per + h) * HD, (g * per + h + 1) * HD)
+                    rows = slice(h * tok + p * part, h * tok + (p + 1) * part)
+                    s = lax.dot_general(q_ref[p * part : (p + 1) * part, at], keys, NT, preferred_element_type=F32) + bias
+                    s_scr[kb, rows] = s
+                    m_scr[rows] = jnp.maximum(
+                        m_scr[rows], jnp.maximum(s[:, :HD], s[:, HD:])
+                    )
 
         for h in range(per):
             rows = slice(h * tok, (h + 1) * tok)
@@ -285,18 +289,20 @@
                 jnp.max(m_scr[rows], axis=1, keepdims=True), (tok, HD)
             )
 
-        @pl.loop(first, last)
-        def _(kb):
-            values = kv_ref[1, pl.ds(pl.multiple_of(kb * step, step), step), lanes]
-            for h in range(per):
-                rows = slice(h * tok, (h + 1) * tok)
-                top = m_scr[rows]
-                s = s_scr[kb, rows]
-                p = jnp.exp2((s - jnp.concatenate([top, top], axis=1)) * scale)
-                l_scr[rows] = l_scr[rows] + (p[:, :HD] + p[:, HD:])
-                a_scr[rows] = a_scr[rows] + jnp.dot(
-                    p.astype(BF), values, preferred_element_type=F32
-                )
+        for p in range(2):
+
+            @pl.loop(*spans[p])
+            def _(kb):
+                values = kv_ref[1, pl.ds(pl.multiple_of(kb * step, step), step), lanes]
+                for h in range(per):
+                    rows = slice(h * tok + p * part, h * tok + (p + 1) * part)
+                    top = m_scr[rows]
+                    s = s_scr[kb, rows]
+                    e = jnp.exp2((s - jnp.concatenate([top, top], axis=1)) * scale)
+                    l_scr[rows] = l_scr[rows] + (e[:, :HD] + e[:, HD:])
+                    a_scr[rows] = a_scr[rows] + jnp.dot(
+                        e.astype(BF), values, preferred_element_type=F32
+                    )
 
         for h in range(per):
             at = slice((g * per + h) * HD, (g * per + h + 1) * HD)

time: 210 us -> 216 us (1.029)
  Pallas kernels: 204 us -> 211 us
    pallas_call x1, Pallas kernels: 165 us -> 171 us  [run_experts(): pl.pallas_call(functools.partial(experts_kernel, nctx, nexp), out_shape=j...]
where the time goes in v4:
time: 216 us
  Pallas kernels  211 us (98%)
  local copies, waits for them, and re-layouts  4.85 us (2%)
    pallas_call x1, Pallas kernels, run_experts(): pl.pallas_call(functools.partial(experts_kernel, nctx, nexp), out_shape=j...  171 us
    pallas_call x1, Pallas kernels, spread(): pl.pallas_call(functools.partial(spread_kernel, nctx), out_shape=(jax.Sha...  25 us
    pallas_call x1, Pallas kernels, attend(): pl.pallas_call(functools.partial(attend_kernel, experts), out_shape=(jax....  13 us
    unnamed x16, local copies, waits for them, and re-layouts  4.85 us

profile of v4, /device:TPU:64, one launch (start us, length us, event | category | flops | bytes accessed | tf_op | source)
XLA Modules:
  0.0 215.8 jit_solution(4148583149195848045)
XLA Ops:
  0.0 0.0 copy-start
  0.0 1.4 copy-done
  1.4 0.0 copy-start.4
  1.4 0.9 copy-done.4
  2.3 0.0 copy-start.6
  2.3 0.7 copy-done.6
  3.0 0.0 copy-start.1
  3.0 25.0 %shard_map.73 = (bf16[2,2048,256]{2,1,0:T(8,128)(2,1)S(1)}, s32[16,1,128]{2,1,0:T(1,128)S(1)}, bf16[80,4096]{1,0:T(8,128)(2,1)S(1)}) custom-call(bf16[2,128,256]{2,1,0:T(8,128)(2,1)S(1)} %bitcast.9, s32[1,128]{1,0:T(1,128)S(1)} %copy-done.6, bf16[192,4096]{1,0:T(8,128)(2,1)S(1)} %bitcast.5), custom_call_target="tpu_custom_call" | custom-call | tf_op jit(solution)/shard_map/pallas_call | solution.py:179
  28.0 0.0 copy-start.2
  28.0 1.2 copy-done.2
  29.2 0.0 copy-start.5
  29.2 0.7 copy-done.5
  29.8 0.0 copy-start.3
  29.8 13.0 %shard_map.74 = (bf16[128,4096]{1,0:T(8,128)(2,1)S(1)}, bf16[256,1024]{1,0:T(8,128)(2,1)S(1)}) custom-call(bf16[2,2048,256]{2,1,0:T(8,128)(2,1)S(1)} %get-tuple-element.10.kv_ref, s32[16,1,128]{2,1,0:T(1,128)S(1)} %get-tuple-element.11.doc_ref, bf16[128,4096]{1,0:T(8,128)(2,1)S(1)} %bitcast.7, s32[1,128]{1,0:T(1,128)S(1)} %copy-done.5), custom_call_target="tpu_custom_call" | custom-call | tf_op jit(solution)/shard_map/pallas_call | solution.py:348
  42.8 0.0 copy-start.7
  42.8 0.0 copy-done.1
  42.8 0.0 copy-done.3
  42.8 171.0 %shard_map.75.back_ref = bf16[256,1024]{1,0:T(8,128)(2,1)S(1)} custom-call(bf16[256,1024]{1,0:T(8,128)(2,1)S(1)} %get-tuple-element.13.send_ref, bf16[192,4096]{1,0:T(8,128)(2,1)S(1)} %bitcast.6, bf16[1536,256]{1,0:T(8,128)(2,1)S(1)} %bitcast.8, bf16[80,4096]{1,0:T(8,128)(2,1)S(1)} %get-tuple-element.14.early_ref), custom_call_target="tpu_custom_call" | custom-call | tf_op jit(solution)/shard_map/pallas_call | solution.py:883
  213.8 0.0 copy-done.7
  213.9 1.8 shard_map.76
Async XLA Ops:
  0.0 1.4 copy-start
  1.4 0.9 copy-start.4
  2.3 0.7 copy-start.6
  3.0 39.9 %copy-start.1 = (bf16[1,2,96,4096]{3,2,1,0:T(8,128)(2,1)S(1)}, bf16[1,2,96,4096]{3,2,1,0:T(8,128)(2,1)}, u32[]{:S(2)}) copy-start(bf16[1,2,96,4096]{3,2,1,0:T(8,128)(2,1)} %param.12) | copy-start | bytes 4718596
  28.0 1.2 copy-start.2
  29.2 0.7 copy-start.5
  29.8 13.0 %copy-start.3 = (bf16[1,1536,256]{2,1,0:T(8,128)(2,1)S(1)}, bf16[1,1536,256]{2,1,0:T(8,128)(2,1)}, u32[]{:S(2)}) copy-start(bf16[1,1536,256]{2,1,0:T(8,128)(2,1)} %param.13) | copy-start | bytes 2359300
  42.8 171.0 %copy-start.7 = (f32[1,128]{1,0:T(1,128)S(1)}, f32[1,128]{1,0:T(1,128)}, u32[]{:S(2)}) copy-start(f32[1,128]{1,0:T(1,128)} %comb_hbm.1) | copy-start | bytes 1540
